TPU v7x, 128 devices: a whole 4x4x4 slice. The times are simulated.
128 devices in a mesh: tm: 8 (over y, core), chan: 16 (over z, x).
Axes of the slice: x: 4, y: 4, z: 4, core: 2. Of those that a mesh axis runs over, the one named last changes fastest.
Arguments:
- samples: float32 [1024, 524288], P('chan', 'tm'), may hold values from -6 to 6
- taps: float32 [1024, 32], P('chan'), may hold values from -1 to 1
- bins: int32 [16], replicated, may hold values from 1 to 127
Outputs:
- csm: float32 [2, 16, 1024, 1024], P(None, None, 'chan', 'tm')
Inputs may be any that keep to these rules, and one draw needn't show every extreme that they name: `bins`: bin numbers of the 256-point transform, repeats possible.
All inputs are finite; a program needn't handle non-finite values.
Results may differ from a plain program's by a relative error of at most 0.0013.
Values may be sent and summed in bfloat16 or wider, within the bound.
No kernel may reach another device: no remote copies, remote signals or barrier semaphores. Data moves between devices by JAX's collectives and lax.ppermute only.
A program may use at most 192 MiB of HBM per device.

v0:
```python
import jax
import jax.numpy as jnp
from jax import lax
from jax.sharding import PartitionSpec as P

SEG = 256


def passed_along(block, axis, distance):
    devices = range(lax.axis_size(axis))
    route = [(i - distance, i) for i in devices if i - distance in devices]
    return lax.ppermute(block, axis, route)


def make_basis(bins):
    index = jnp.arange(SEG, dtype=jnp.int32)
    window = 0.5 - 0.5 * jnp.cos(2.0 * jnp.pi * index.astype(jnp.float32) / SEG)
    phase_int = index[:, None] * bins[None, :] % SEG
    phase = 2.0 * jnp.pi * phase_int.astype(jnp.float32) / SEG
    return jnp.stack([window[:, None] * jnp.cos(phase), -window[:, None] * jnp.sin(phase)], axis=2)


def equalize(extended, taps, out_len):
    ntap = taps.shape[1]
    total = jnp.zeros((extended.shape[0], out_len), jnp.float32)
    for k in range(ntap):
        total = total + taps[:, k][:, None] * extended[:, ntap - 1 - k : ntap - 1 - k + out_len]
    return total


def body(samples, taps, bins):
    width = samples.shape[0]
    span = samples.shape[1]
    ntap = taps.shape[1]
    hop = SEG // 2
    tail = passed_along(samples[:, span - (ntap - 1) :], "tm", 1)
    filtered = equalize(jnp.concatenate([tail, samples], axis=1), taps, span)
    before = passed_along(filtered[:, span - hop :].astype(jnp.bfloat16), "tm", 1).astype(
        jnp.float32
    )
    framed = jnp.concatenate([before, filtered], axis=1)
    basis = make_basis(bins)
    pieces = framed.reshape(width, span // hop + 1, hop)
    own = jnp.einsum("cjh,hbp->bpcj", pieces[:, :-1], basis[:hop], precision=lax.Precision.HIGHEST)
    own = own + jnp.einsum(
        "cjh,hbp->bpcj", pieces[:, 1:], basis[hop:], precision=lax.Precision.HIGHEST
    )
    own = own.astype(jnp.bfloat16)
    segments_all = lax.axis_size("tm") * (span // hop)
    scale = 1.0 / (segments_all * 3.0 * SEG / 8.0)
    prod = jnp.einsum(
        "bpis,bqjs->bpqij",
        own,
        lax.all_gather(own, "chan", axis=2, tiled=True),
        preferred_element_type=jnp.float32,
    )
    real_part = prod[:, 0, 0] + prod[:, 1, 1]
    imag_part = prod[:, 1, 0] - prod[:, 0, 1]
    term = jnp.stack([real_part, imag_part], axis=0) * scale
    columns = term.shape[3] // lax.axis_size("tm")
    summed = lax.psum(term, "tm")
    result = lax.dynamic_slice_in_dim(summed, lax.axis_index("tm") * columns, columns, 3)
    return result


def solution(mesh):
    return jax.shard_map(
        body,
        mesh=mesh,
        in_specs=(P("chan", "tm"), P("chan", None), P()),
        out_specs=P(None, None, "chan", "tm"),
        check_vma=False,
    )
```

profile of v0, /device:TPU:0, one launch (start us, length us, event | category | flops | bytes accessed | tf_op | source)
XLA Modules:
  0.0 792.7 jit_solution(15471069479135969734)
XLA Ops:
  6.5 0.0 all-gather.2.cloned.1.call-start
  6.5 0.8 slice.223
  7.4 1.3 collective-permute-start
  8.7 1.1 slice_bitcast_fusion.39
  9.7 1.0 slice_bitcast_fusion.38
  10.8 0.0 collective-permute-done
  10.8 0.0 copy-start.1
  10.8 324.8 %fusion.5 = f32[64,65536]{1,0:T(8,128)S(1)} fusion(f32[64,31]{1,0:T(8,128)S(1)} %collective-permute-done, f32[64,65536]{1,0:T(8,128)} %param.3, f32[64]{0:T(128)S(1)} %get-tuple-element.35, f32[64]{0:T(128)S(1)} %get-tuple-element.36, f32[64]{0:T(128)S(1)} %get-tuple-element.6, f32[64]{0:T(128)S(1)} %get-tuple-element.7, f32[64]{0:T(128)S(1)} %get-tuple-element.8, ...), kind=kLoop, calls=%fused_computation.36 | loop fusion | flops 394264576 | bytes 33570560 | tf_op jit(solution)/shard_map/add | solution.py:27
  335.6 4.6 collective-permute-start.1
  340.2 0.0 copy-done.1
  340.2 0.2 cosine_multiply_fusion
  340.4 0.4 collective-permute-done.1
  340.8 6.0 pad_maximum_fusion
  346.8 14.4 %reshape.192 = f32[64,513,128]{2,1,0:T(8,128)} reshape(f32[64,65664]{1,0:T(8,128)} %pad_maximum_fusion) | data formatting | bytes 33619968 | tf_op jit(solution)/shard_map/reshape | solution.py:43
  361.2 0.0 copy-start
  361.2 22.1 %fusion.93 = f32[16,2,64,512]{3,0,2,1:T(8,128)S(1)} fusion(f32[64,513,128]{2,1,0:T(8,128)} %reshape.192, f32[256,16,1]{0,1,2:T(8,128)S(1)} %get-tuple-element.38, f32[256,16,1]{0,1,2:T(8,128)S(1)} %get-tuple-element.37), kind=kOutput, calls=%fused_computation.125 | convolution fusion | flops 1610616832 | bytes 21004288 | tf_op jit(solution)/shard_map/cjh,hbp->bpcj/dot_general | solution.py:45
  383.3 0.0 copy-done
  383.3 18.4 %add_convert_fusion = bf16[16,2,64,512]{3,0,2,1:T(8,128)(2,1)} fusion(f32[16,2,64,512]{3,0,2,1:T(8,128)S(1)} %fusion.93, f32[64,513,128]{2,1,0:T(8,128)S(1)} %copy-done, f32[256,16,1]{0,1,2:T(8,128)S(1)} %get-tuple-element.37, f32[256,16,1]{0,1,2:T(8,128)S(1)} %get-tuple-element.38), kind=kOutput, calls=%fused_computation.146 | convolution fusion | flops 1612713984 | bytes 23101440 | tf_op jit(solution)/shard_map/cjh,hbp->bpcj/dot_general | solution.py:44
  401.7 0.0 all-gather.2.cloned.1.call-update
  401.7 0.0 all-reduce.2.cloned.1.call-start
  401.8 201.5 %all-gather.2.cloned.1.call-done = bf16[16,2,1024,512]{3,0,2,1:T(8,128)(2,1)} async-done(((bf16[16,2,64,512]{3,0,2,1:T(8,128)(2,1)}), bf16[16,2,1024,512]{3,0,2,1:T(8,128)(2,1)}) %all-gather.2.cloned.1.call-update) | async-done | bytes 33554448 | tf_op jit(solution)/shard_map/all_gather | solution.py:54
  603.3 63.2 %fusion.96 = f32[16,2,2,64,1024]{4,3,1,2,0:T(8,128)} fusion(bf16[16,2,1024,512,1]{3,0,2,1,4:T(8,128)(2,1)} %bitcast.100, bf16[16,2,64,512,1]{3,0,2,1,4:T(8,128)(2,1)} %bitcast.101), kind=kOutput, calls=%fused_computation.138 | convolution fusion | flops 4294967296 | bytes 52428800 | tf_op jit(solution)/shard_map/bpis,bqjs->bpqij/dot_general | solution.py:51
  666.5 4.4 fusion.101
  670.9 4.4 fusion.99
  675.3 4.3 maximum_multiply_fusion
  679.6 0.0 all-reduce.2.cloned.1.call-update
  679.6 103.7 %all-reduce.2.cloned.1.call-done = f32[2,16,64,1024]{3,2,1,0:T(8,128)} async-done(((f32[2,16,64,1024]{3,2,1,0:T(8,128)}), f32[2,16,64,1024]{3,2,1,0:T(8,128)}) %all-reduce.2.cloned.1.call-update) | async-done | bytes 8388624 | tf_op jit(solution)/shard_map/psum | solution.py:61
  783.3 2.3 constant_dynamic-slice_fusion
  (3 shorter events, 0.1 us)
Async XLA Ops:
  6.5 596.7 %all-gather.2.cloned.1.call-start = ((), (), s32[]{:S(2)}) async-start(), calls=%async_computation | async-start | bytes 35651584 | tf_op jit(solution)/shard_map/all_gather | solution.py:54
  7.4 3.4 collective-permute-start
  10.8 329.5 %copy-start.1 = (s32[16]{0:T(128)S(1)}, s32[16]{0:T(128)}, u32[]{:S(2)}) copy-start(s32[16]{0:T(128)} %param.5) | copy-start | bytes 196
  335.6 5.1 collective-permute-start.1
  361.2 22.1 %copy-start = (f32[64,513,128]{2,1,0:T(8,128)S(1)}, f32[64,513,128]{2,1,0:T(8,128)}, u32[]{:S(2)}) copy-start(f32[64,513,128]{2,1,0:T(8,128)} %reshape.192) | copy-start | bytes 50429956
  401.7 381.6 %all-reduce.2.cloned.1.call-start = ((), (), s32[]{:S(2)}) async-start(), calls=%async_computation.1 | async-start | bytes 16777216 | tf_op jit(solution)/shard_map/psum | solution.py:61
Sparse Core Ops, SparseCore 0:
  401.9 201.3 all-gather.1
  679.7 103.5 all-reduce.1
where the time goes:
time: 798 us; the launch traced here: 793 us
  other arithmetic  344 us (43%)
  waiting for transfers between devices  306 us (38%)
  matrix products  104 us (13%)
  local copies, waits for them, and re-layouts  19.6 us (2%)
  between operations  13.7 us (2%)
    add x1, other arithmetic, equalize(): total + taps[:, k][:, None] * extended[:, ntap - 1 - k:ntap - 1 - k + out...  325 us
    all_gather x1, waiting for transfers between devices, body(): lax.all_gather(own, 'chan', axis=2, tiled=True)  201 us
    psum x1, waiting for transfers between devices, body(): summed = lax.psum(term, 'tm')  104 us
    dot_general x1, matrix products, body(): jnp.einsum('bpis,bqjs->bpqij', own, lax.all_gather(own, 'chan', axis=2, t...  63.2 us
    dot_general x1, matrix products, body(): jnp.einsum('cjh,hbp->bpcj', pieces[:, 1:], basis[hop:], precision=lax.Pre...  22.1 us
    dot_general x1, matrix products, body(): jnp.einsum('cjh,hbp->bpcj', pieces[:, :-1], basis[:hop], precision=lax.Pr...  18.4 us
  transfers between devices with their start and end apart: 4, of which 3 were waited for; matrix products, arithmetic and copies ran while one was open for 0% of the time, Pallas kernels for 0%

commit v1 on v0

v1 whole, which is shorter than its diff:
```python
import functools

import jax
import jax.numpy as jnp
from jax import lax
from jax.experimental import pallas as pl
from jax.experimental.pallas import tpu as pltpu
from jax.sharding import PartitionSpec as P

SEG = 256
HOP = 128
NT = (((1,), (1,)), ((), ()))


def passed_along(block, axis, distance):
    devices = range(lax.axis_size(axis))
    route = [(i - distance, i) for i in devices if i - distance in devices]
    return lax.ppermute(block, axis, route)


def make_basis_rows(bins):
    index = jnp.arange(SEG, dtype=jnp.int32)
    window = 0.5 - 0.5 * jnp.cos(2.0 * jnp.pi * index.astype(jnp.float32) / SEG)
    phase_int = bins[:, None] * index[None, :] % SEG
    phase = 2.0 * jnp.pi * phase_int.astype(jnp.float32) / SEG
    rows = jnp.stack([window * jnp.cos(phase), -window * jnp.sin(phase)], axis=1)
    return rows.reshape(2 * bins.shape[0], SEG)


def tap_basis(taps, bins):
    ntap = taps.shape[1]
    rows = make_basis_rows(bins)
    ext = jnp.pad(rows, ((0, 0), (HOP, ntap - 1)))
    shifted = jnp.stack([ext[:, k : k + 3 * HOP] for k in range(ntap)])
    return jnp.einsum("ck,krq->crq", taps, shifted, precision=lax.Precision.HIGHEST)


def split(value):
    high = value.astype(jnp.bfloat16)
    return high, (value - high.astype(jnp.float32)).astype(jnp.bfloat16)


def spectra_kernel(x_ref, h_ref, v_ref, o_ref, s_ref):
    nrow = o_ref.shape[0]
    nseg = o_ref.shape[2]
    lane = lax.broadcasted_iota(jnp.int32, (nrow, nseg), 1)
    for c in range(16):
        g, r = divmod(c, 8)
        x = x_ref[g, pl.ds(r, nseg, stride=8), :]
        data = jnp.concatenate(split(x), axis=1)
        v = v_ref[c]
        vh, vl = split(v)
        high = jnp.concatenate([vh[:, i * HOP : (i + 1) * HOP] for i in range(3)], axis=0)
        low = jnp.concatenate([vl[:, i * HOP : (i + 1) * HOP] for i in range(3)], axis=0)
        weights = jnp.concatenate(
            [
                jnp.concatenate([high, high], axis=1),
                jnp.concatenate([low, jnp.zeros_like(low)], axis=1),
            ],
            axis=0,
        )
        z = lax.dot_general(weights, data, NT, preferred_element_type=jnp.float32)
        z = z[: 3 * nrow] + z[3 * nrow :]
        older = h_ref[g, r : r + 1, :]
        newer = h_ref[g, 8 + r : 9 + r, :]
        first = jnp.sum(v[:, HOP : 2 * HOP] * newer + v[:, :HOP] * older, axis=1, keepdims=True)
        second = jnp.sum(v[:, :HOP] * newer, axis=1, keepdims=True)
        z1 = jnp.where(lane == 0, first, pltpu.roll(z[nrow : 2 * nrow], 1, 1))
        z0 = jnp.where(lane == 1, second, pltpu.roll(z[:nrow], 2, 1))
        z0 = jnp.where(lane == 0, 0.0, z0)
        total = z[2 * nrow :] + z1 + z0
        for i in range(nseg // 128):
            s_ref[i, pl.ds(c, nrow, stride=16), :] = total[:, i * 128 : (i + 1) * 128]
    for j in range(nrow):
        for i in range(nseg // 128):
            part = s_ref[i, j * 16 : (j + 1) * 16, :]
            o_ref[j, :, i * 128 : (i + 1) * 128] = part.astype(jnp.bfloat16)


def spectra(samples, before, weights):
    width, span = samples.shape
    nseg = span // HOP
    nrow = weights.shape[1]

    def by_rows(a):
        n = a.shape[1] // HOP
        return a.reshape(width // 8, 8, n, HOP).transpose(0, 2, 1, 3).reshape(width // 8, n * 8, HOP)

    return pl.pallas_call(
        spectra_kernel,
        grid=(width // 16,),
        in_specs=[
            pl.BlockSpec((2, nseg * 8, HOP), lambda i: (i, 0, 0)),
            pl.BlockSpec((2, 16, HOP), lambda i: (i, 0, 0)),
            pl.BlockSpec((16, nrow, 3 * HOP), lambda i: (i, 0, 0)),
        ],
        out_specs=pl.BlockSpec((nrow, 16, nseg), lambda i: (0, i, 0)),
        out_shape=jax.ShapeDtypeStruct((nrow, width, nseg), jnp.bfloat16),
        scratch_shapes=[pltpu.VMEM((nseg // 128, nrow * 16, 128), jnp.float32)],
        compiler_params=pltpu.CompilerParams(vmem_limit_bytes=48 * 2**20),
        cost_estimate=pl.CostEstimate(
            flops=2 * 2 * 6 * nrow * width * span, bytes_accessed=width * span * 4, transcendentals=0
        ),
        name="spectra",
    )(by_rows(samples), by_rows(before), weights)


def csm_kernel(scale, x_ref, o_ref):
    nsrc, _, width, nseg = x_ref.shape
    take = 256 // width
    j = pl.program_id(0)
    real = x_ref[:, 0].reshape(nsrc * width, nseg)
    imag = x_ref[:, 1].reshape(nsrc * width, nseg)
    cols = x_ref[pl.ds(j * take, take)]
    creal = cols[:, 0].reshape(256, nseg)
    cimag = cols[:, 1].reshape(256, nseg)

    def dot(a, b):
        return lax.dot_general(a, b, NT, preferred_element_type=jnp.float32)

    re = (dot(real, creal) + dot(imag, cimag)) * scale
    for i in range(2):
        o_ref[i, :, 0] = re[:, i * 128 : (i + 1) * 128].reshape(nsrc, width, 128)
    im = (dot(imag, creal) - dot(real, cimag)) * scale
    for i in range(2):
        o_ref[i, :, 1] = im[:, i * 128 : (i + 1) * 128].reshape(nsrc, width, 128)


def csm_partial(x, scale):
    nsrc, _, width, nseg = x.shape
    chans = nsrc * width
    return pl.pallas_call(
        functools.partial(csm_kernel, scale),
        grid=(chans // 256,),
        in_specs=[pl.BlockSpec(x.shape, lambda j: (0, 0, 0, 0))],
        out_specs=pl.BlockSpec((2, nsrc, 2, width, 128), lambda j: (j, 0, 0, 0, 0)),
        out_shape=jax.ShapeDtypeStruct((chans // 128, nsrc, 2, width, 128), jnp.float32),
        compiler_params=pltpu.CompilerParams(vmem_limit_bytes=48 * 2**20),
        cost_estimate=pl.CostEstimate(
            flops=8 * chans * chans * nseg, bytes_accessed=chans * chans * 8, transcendentals=0
        ),
        name="csm",
    )(x)


def body(samples, taps, bins):
    width, span = samples.shape
    nbin = bins.shape[0]
    before = passed_along(samples[:, span - SEG :], "tm", 1)
    own = spectra(samples, before, tap_basis(taps, bins))
    own = own.reshape(nbin, 2, width, span // HOP)
    mine = lax.all_to_all(own, "chan", 0, 0)
    segments_all = lax.axis_size("tm") * (span // HOP)
    partial = csm_partial(mine, 1.0 / (segments_all * 3.0 * SEG / 8.0))
    summed = lax.psum_scatter(partial, "tm", scatter_dimension=0)
    rows = lax.all_to_all(summed, "chan", 0, 0)
    return rows.transpose(1, 0, 2, 3)


def solution(mesh):
    return jax.shard_map(
        body,
        mesh=mesh,
        in_specs=(P("chan", "tm"), P("chan", None), P()),
        out_specs=P(None, None, "chan", "tm"),
        check_vma=False,
    )
```

time: 798 us -> 158 us (0.20)
  other arithmetic: 344 us -> 0.86 us
  waiting for transfers between devices: 306 us -> 51.6 us
  matrix products: 104 us -> 2.69 us
  blocking collectives: 0 us -> 61.1 us
  Pallas kernels: 0 us -> 17.3 us
  local copies, waits for them, and re-layouts: 19.6 us -> 8.8 us
    add x2 -> x0, other arithmetic: 329 us -> none  [the longest x1 325 us: equalize(): total + taps[:, k][:, None] * extended[:, ntap - 1 - k:ntap - 1 - k + out...]
    all_gather x1 -> x0, waiting for transfers between devices: 201 us -> none  [body(): lax.all_gather(own, 'chan', axis=2, tiled=True)]
    psum x1 -> x0, waiting for transfers between devices: 104 us -> none  [body(): summed = lax.psum(term, 'tm')]
    dot_general x3 -> x1, matrix products: 104 us -> 2.69 us  [tap_basis(): jnp.einsum('ck,krq->crq', taps, shifted, precision=lax.Precision.HIGHEST)]
    all_to_all x0 -> x2, blocking collectives: none -> 61.1 us  [the longest x1 37.6 us: body(): mine = lax.all_to_all(own, 'chan', 0, 0)]
    reduce_scatter x0 -> x1, waiting for transfers between devices: none -> 51.6 us  [body(): summed = lax.psum_scatter(partial, 'tm', scatter_dimension=0)]
    pallas_call x0 -> x2, Pallas kernels: none -> 17.3 us  [the longest x1 10.7 us: spectra(): pl.pallas_call(spectra_kernel, grid=(width // 16,), in_specs=[pl.BlockSpe...]
    reshape x1, local copies, waits for them, and re-layouts: 14.4 us -> 0.02 us  [make_basis_rows(): return rows.reshape(2 * bins.shape[0], SEG)]
  transfers between devices with their start and end apart: 4 -> 2, of which waited for: 3 -> 1; matrix products, arithmetic and copies ran while one was open for 0% -> 7% of each run, Pallas kernels for 0% -> 0%
where the time goes in v1:
time: 158 us; the launch traced here: 157 us
  blocking collectives  61.1 us (39%)
  waiting for transfers between devices  51.6 us (33%)
  Pallas kernels  17.3 us (11%)
  between operations  13.7 us (9%)
  local copies, waits for them, and re-layouts  8.8 us (6%)
  matrix products  2.69 us (2%)
    reduce_scatter x1, waiting for transfers between devices, body(): summed = lax.psum_scatter(partial, 'tm', scatter_dimension=0)  51.6 us
    all_to_all x1, blocking collectives, body(): mine = lax.all_to_all(own, 'chan', 0, 0)  37.6 us
    all_to_all x1, blocking collectives, body(): rows = lax.all_to_all(summed, 'chan', 0, 0)  23.5 us
    pallas_call x1, Pallas kernels, spectra(): pl.pallas_call(spectra_kernel, grid=(width // 16,), in_specs=[pl.BlockSpe...  10.7 us
    pallas_call x1, Pallas kernels, csm_partial(): pl.pallas_call(functools.partial(csm_kernel, scale), grid=(chans // 256,)...  6.57 us
    another operation x34, local copies, waits for them, and re-layouts, tap_basis(): shifted = jnp.stack([ext[:, k:k + 3 * HOP] for k in range(ntap)])  4.67 us
  transfers between devices with their start and end apart: 2, of which 1 were waited for; matrix products, arithmetic and copies ran while one was open for 7% of the time, Pallas kernels for 0%

profile of v1, /device:TPU:0, one launch (start us, length us, event | category | flops | bytes accessed | tf_op | source)
XLA Modules:
  0.0 157.4 jit_solution(2888987177355346708)
XLA Ops:
  6.5 0.0 copy-start
  6.5 0.9 slice.99
  7.4 1.3 collective-permute-start
  8.7 0.8 cosine_multiply_fusion
  9.6 0.2 fusion.30
  9.8 0.3 pad_slice_fusion
  10.2 0.1 copy.101
  10.2 0.1 copy.90
  10.3 0.1 copy.91
  10.3 0.1 copy.92
  10.4 0.1 copy.93
  10.5 0.1 copy.94
  10.5 0.1 copy.95
  10.6 0.1 copy.96
  10.6 0.1 copy.97
  10.7 0.1 copy.98
  10.8 0.1 copy.99
  10.8 0.1 copy.100
  10.9 0.1 copy.71
  11.0 0.1 copy.72
  11.0 0.1 copy.73
  11.1 0.1 copy.74
  11.2 0.1 copy.75
  11.2 0.1 copy.76
  11.3 0.1 copy.77
  11.3 0.1 copy.78
  11.4 0.1 copy.79
  11.5 0.1 copy.80
  11.5 0.1 copy.81
  11.6 0.1 copy.82
  11.6 0.1 copy.83
  11.7 0.1 copy.84
  11.8 0.1 copy.85
  11.8 0.1 copy.86
  11.9 0.1 copy.87
  11.9 0.1 copy.88
  12.0 0.1 copy.89
  12.1 2.8 %stack.137 = f32[32,32,384]{2,0,1:T(8,128)S(1)} concatenate(f32[1,32,384]{2,0,1:T(1,128)S(1)} %copy.71, f32[1,32,384]{2,0,1:T(1,128)S(1)} %copy.72, f32[1,32,384]{2,0,1:T(1,128)S(1)} %copy.73, f32[1,32,384]{2,0,1:T(1,128)S(1)} %copy.74, f32[1,32,384]{2,0,1:T(1,128)S(1)} %copy.75, f32[1,32,384]{2,0,1:T(1,128)S(1)} %copy.76, f32[1,32,384]{2,0,1:T(1,128)S(1)} %copy.77, ...), dimensions={0} | concatenate | bytes 3145728 | tf_op jit(solution)/shard_map/stack | solution.py:34
  14.9 2.7 %fusion.34 = f32[32,384,64]{1,2,0:T(8,128)S(1)} fusion(f32[32,32,384]{2,0,1:T(8,128)S(1)} %stack.137, f32[64,32]{0,1:T(8,128)S(1)} %copy-done), kind=kOutput, calls=%fused_computation.71 | convolution fusion | flops 301989888 | bytes 4726784 | tf_op jit(solution)/shard_map/ck,krq->crq/dot_general | solution.py:35
  17.6 1.8 %copy.105 = f32[32,384,64]{1,0,2:T(8,128)S(1)} copy(f32[32,384,64]{1,2,0:T(8,128)S(1)} %fusion.34) | data formatting | bytes 6291456 | tf_op jit(solution)/shard_map/ck,krq->crq/dot_general | solution.py:35
  19.4 0.0 collective-permute-done
  19.4 10.7 %spectra.1 = bf16[32,64,512]{2,1,0:T(8,128)(2,1)S(1)} custom-call(f32[8,4096,128]{2,1,0:T(8,128)} %bitcast.85, f32[8,16,128]{2,1,0:T(8,128)S(1)} %bitcast.84, f32[64,32,384]{2,1,0:T(8,128)S(1)} %bitcast.82), custom_call_target="tpu_custom_call" | custom-call | flops 3221225472 | bytes 16777216 | tf_op jit(solution)/shard_map/spectra/pallas_call | solution.py:89
  30.2 37.6 %all_to_all.10.x_ref = bf16[16,2,64,512]{3,2,1,0:T(8,128)(2,1)S(1)} all-to-all(bf16[16,2,64,512]{3,2,1,0:T(8,128)(2,1)S(1)} %bitcast.83), channel_id=1, replica_groups=mesh['tm'=8,'chan'=16] {'chan'}, dimensions={0} | all-to-all | bytes 4194304 | tf_op jit(solution)/shard_map/all_to_all | solution.py:152
  67.8 6.6 %csm.1 = f32[8,16,2,64,128]{4,3,2,1,0:T(8,128)} custom-call(bf16[16,2,64,512]{3,2,1,0:T(8,128)(2,1)S(1)} %all_to_all.10.x_ref), custom_call_target="tpu_custom_call" | custom-call | flops 4294967296 | bytes 8388608 | tf_op jit(solution)/shard_map/csm/pallas_call | solution.py:132
  74.3 0.0 reduce-scatter.2.cloned.1.call-update
  74.3 51.6 %reduce-scatter.2.cloned.1.call-done = f32[1,16,2,64,128]{4,3,2,1,0:T(8,128)} async-done(((f32[8,16,2,64,128]{4,3,2,1,0:T(8,128)}), f32[1,16,2,64,128]{4,3,2,1,0:T(8,128)}) %reduce-scatter.2.cloned.1.call-update) | async-done | bytes 1048592 | tf_op jit(solution)/shard_map/reduce_scatter | solution.py:155
  125.9 23.5 %all_to_all.11 = f32[16,2,64,128]{3,2,1,0:T(8,128)S(1)} all-to-all(f32[16,2,64,128]{3,2,1,0:T(8,128)} %bitcast.87), channel_id=1, replica_groups=mesh['tm'=8,'chan'=16] {'chan'}, dimensions={0} | all-to-all | bytes 2097152 | tf_op jit(solution)/shard_map/all_to_all | solution.py:156
  149.5 1.1 copy.103
  (7 shorter events, 0.1 us)
Async XLA Ops:
  6.5 8.3 %copy-start = (f32[64,32]{0,1:T(8,128)S(1)}, f32[64,32]{0,1:T(8,128)}, u32[]{:S(2)}) copy-start(f32[64,32]{0,1:T(8,128)} %param.4) | copy-start | bytes 24580
  6.5 119.4 %reduce-scatter.2.cloned.1.call-start = ((), (), s32[]{:S(2)}) async-start(), calls=%async_computation.3 | async-start | bytes 9437184 | tf_op jit(solution)/shard_map/reduce_scatter | solution.py:155
  7.4 12.0 %collective-permute-start = (f32[64,256]{1,0:T(8,128)S(1)}, f32[64,256]{1,0:T(8,128)S(1)}, u32[]{:S(2)}, u32[]{:S(2)}) collective-permute-start(f32[64,256]{1,0:T(8,128)S(1)} %slice.99), channel_id=1, source_target_pairs={{0,16},{16,32},{32,48},{48,64},{64,80},{80,96},{96,112},{1,17},{17... | collective-permute-start | bytes 196616 | tf_op jit(solution)/shard_map/ppermute | solution.py:18
Sparse Core Ops, SparseCore 0:
  74.5 51.4 reduce-scatter.1

commit v2 on v1

v2 whole, which is shorter than its diff:
```python
import functools

import jax
import jax.numpy as jnp
from jax import lax
from jax.experimental import pallas as pl
from jax.experimental.pallas import tpu as pltpu
from jax.sharding import PartitionSpec as P

SEG = 256
HOP = 128
CODE = 32700.0
LEVELS = 64.0
NT = (((1,), (1,)), ((), ()))


def passed_along(block, axis, distance):
    devices = range(lax.axis_size(axis))
    route = [(i - distance, i) for i in devices if i - distance in devices]
    return lax.ppermute(block, axis, route)


def make_basis_rows(bins):
    index = jnp.arange(SEG, dtype=jnp.int32)
    window = 0.5 - 0.5 * jnp.cos(2.0 * jnp.pi * index.astype(jnp.float32) / SEG)
    phase_int = bins[:, None] * index[None, :] % SEG
    phase = 2.0 * jnp.pi * phase_int.astype(jnp.float32) / SEG
    rows = jnp.stack([window * jnp.cos(phase), -window * jnp.sin(phase)], axis=1)
    return rows.reshape(2 * bins.shape[0], SEG)


def weights_kernel(t_ref, b_ref, o_ref):
    nrow = b_ref.shape[0]
    width, ntap = t_ref.shape
    size = b_ref.shape[1]
    th, tl = split(t_ref[...])
    lhs = jnp.concatenate([th, tl, th], axis=1)
    for row in range(nrow):
        line = jnp.broadcast_to(b_ref[row : row + 1, :], (ntap, size))
        line = pltpu.roll(line, size - ntap + 1, 1, stride=1, stride_axis=0)
        high, low = split(line[:, : 3 * HOP])
        rhs = jnp.concatenate([high, high, low], axis=0)
        out = jnp.dot(lhs, rhs, preferred_element_type=jnp.float32)
        for g in range(3):
            for i in range(width // 8):
                part = out[i * 8 : (i + 1) * 8, g * HOP : (g + 1) * HOP]
                o_ref[g, pl.ds(i * 8 * nrow + row, 8, stride=nrow), :] = part


def tap_basis(taps, bins):
    width, ntap = taps.shape
    nrow = 2 * bins.shape[0]
    ext = jnp.pad(make_basis_rows(bins), ((0, 0), (HOP, HOP)))
    return pl.pallas_call(
        weights_kernel,
        out_shape=jax.ShapeDtypeStruct((3, width * nrow, HOP), jnp.float32),
        compiler_params=pltpu.CompilerParams(vmem_limit_bytes=32 * 2**20),
        cost_estimate=pl.CostEstimate(
            flops=18 * ntap * nrow * width * HOP,
            bytes_accessed=12 * width * nrow * HOP,
            transcendentals=0,
        ),
        name="weights",
    )(taps[:, ::-1], ext)


def split(value):
    high = value.astype(jnp.bfloat16)
    return high, (value - high.astype(jnp.float32)).astype(jnp.bfloat16)


def spectra_kernel(x_ref, h_ref, v_ref, o_ref, s_ref):
    nrow = 2 * o_ref.shape[0]
    nseg = o_ref.shape[2] // 2
    lane = lax.broadcasted_iota(jnp.int32, (nrow, nseg), 1)
    for c in range(16):
        g, r = divmod(c, 8)
        x = x_ref[g, pl.ds(r, nseg, stride=8), :]
        data = jnp.concatenate(split(x), axis=1)
        v = v_ref[:, c * nrow : (c + 1) * nrow, :]
        high, low = split(v.reshape(3 * nrow, HOP))
        weights = jnp.concatenate(
            [
                jnp.concatenate([high, high], axis=1),
                jnp.concatenate([low, jnp.zeros_like(low)], axis=1),
            ],
            axis=0,
        )
        z = lax.dot_general(weights, data, NT, preferred_element_type=jnp.float32)
        z = z[: 3 * nrow] + z[3 * nrow :]
        older = h_ref[g, r : r + 1, :]
        newer = h_ref[g, 8 + r : 9 + r, :]
        first = jnp.sum(v[1] * newer + v[0] * older, axis=1, keepdims=True)
        second = jnp.sum(v[0] * newer, axis=1, keepdims=True)
        z1 = jnp.where(lane == 0, first, pltpu.roll(z[nrow : 2 * nrow], 1, 1))
        z0 = jnp.where(lane == 1, second, pltpu.roll(z[:nrow], 2, 1))
        z0 = jnp.where(lane == 0, 0.0, z0)
        total = z[2 * nrow :] + z1 + z0
        for i in range(nseg // 128):
            s_ref[i, pl.ds(c, nrow, stride=16), :] = total[:, i * 128 : (i + 1) * 128]
    for j in range(nrow):
        for i in range(nseg // 128):
            part = s_ref[i, j * 16 : (j + 1) * 16, :]
            at = j % 2 * nseg + i * 128
            o_ref[j // 2, :, at : at + 128] = part.astype(jnp.bfloat16)


def spectra(samples, before, weights):
    width, span = samples.shape
    nseg = span // HOP
    nrow = weights.shape[1] // width

    def by_rows(a):
        n = a.shape[1] // HOP
        return a.reshape(width // 8, 8, n, HOP).transpose(0, 2, 1, 3).reshape(width // 8, n * 8, HOP)

    return pl.pallas_call(
        spectra_kernel,
        grid=(width // 16,),
        in_specs=[
            pl.BlockSpec((2, nseg * 8, HOP), lambda i: (i, 0, 0)),
            pl.BlockSpec((2, 16, HOP), lambda i: (i, 0, 0)),
            pl.BlockSpec((3, 16 * nrow, HOP), lambda i: (0, i, 0)),
        ],
        out_specs=pl.BlockSpec((nrow // 2, 16, 2 * nseg), lambda i: (0, i, 0)),
        out_shape=jax.ShapeDtypeStruct((nrow // 2, width, 2 * nseg), jnp.bfloat16),
        scratch_shapes=[pltpu.VMEM((nseg // 128, nrow * 16, 128), jnp.float32)],
        compiler_params=pltpu.CompilerParams(vmem_limit_bytes=48 * 2**20),
        cost_estimate=pl.CostEstimate(
            flops=2 * 2 * 6 * nrow * width * span, bytes_accessed=width * span * 4, transcendentals=0
        ),
        name="spectra",
    )(by_rows(samples), by_rows(before), weights)


def csm_kernel(core_ref, own_ref, other_ref, o_ref, p_ref):
    nsrc, width, depth = own_ref.shape
    nseg = depth // 2
    blocks = o_ref.shape[0]
    chans = nsrc * width
    take = HOP // width
    core = core_ref[0]
    largest = jnp.zeros((1, 2 * HOP), jnp.float32)
    for y in range(blocks):
        at = (2 * y + core) * take

        def columns(ref):
            cols = ref[pl.ds(at, take)].reshape(HOP, depth)
            turned = jnp.concatenate([-cols[:, nseg:], cols[:, :nseg]], axis=1)
            return jnp.concatenate([cols, turned], axis=0)

        own, other = columns(own_ref), columns(other_ref)
        for r in range(0, nsrc, 4):
            rows = pl.ds(r * width, 4 * width)
            part = lax.dot_general(
                own_ref[r : r + 4].reshape(4 * width, depth),
                own,
                NT,
                preferred_element_type=jnp.float32,
            ) + lax.dot_general(
                other_ref[r : r + 4].reshape(4 * width, depth),
                other,
                NT,
                preferred_element_type=jnp.float32,
            )
            p_ref[y, rows, :] = part
            largest = jnp.maximum(largest, jnp.max(jnp.abs(part), axis=0, keepdims=True))
    top = jnp.max(largest, axis=1, keepdims=True)
    level = jnp.ceil(jnp.log2(jnp.maximum(top, 1e-30)) * LEVELS)
    gain = CODE * CODE * jnp.exp2(level * (-1.0 / LEVELS))
    mark = jnp.broadcast_to(level, (16, HOP)).astype(jnp.int32).astype(jnp.int16)
    for y in range(blocks):
        for r in range(nsrc):
            part = p_ref[y, r * width : (r + 1) * width, :]
            code = (jnp.sqrt(jnp.abs(part) * gain) + 0.5).astype(jnp.int32)
            code = jnp.where(part < 0.0, -code, code).astype(jnp.int16)
            o_ref[y, r, :width] = code[:, :HOP]
            o_ref[y, r, width : 2 * width] = code[:, HOP:]
            o_ref[y, r, 2 * width :] = mark


def csm_codes(core, own, other, blocks):
    nsrc, width, depth = own.shape
    chans = nsrc * width
    return pl.pallas_call(
        csm_kernel,
        in_specs=[
            pl.BlockSpec(memory_space=pltpu.SMEM),
            pl.BlockSpec(memory_space=pltpu.VMEM),
            pl.BlockSpec(memory_space=pltpu.VMEM),
        ],
        out_specs=pl.BlockSpec(memory_space=pltpu.VMEM),
        out_shape=jax.ShapeDtypeStruct((blocks, nsrc, 2 * width + 16, HOP), jnp.int16),
        scratch_shapes=[pltpu.VMEM((blocks, chans, 2 * HOP), jnp.float32)],
        compiler_params=pltpu.CompilerParams(vmem_limit_bytes=48 * 2**20),
        cost_estimate=pl.CostEstimate(
            flops=8 * chans * blocks * HOP * depth,
            bytes_accessed=4 * chans * (depth + blocks * HOP),
            transcendentals=0,
        ),
        name="csm",
    )(core, own, other)


def total_kernel(scale, c_ref, o_ref):
    blocks, nbin, _, _ = c_ref.shape
    width = o_ref.shape[2]
    for b in range(nbin):
        total = jnp.zeros((2 * width, HOP), jnp.float32)
        for y in range(blocks):
            mark = c_ref[y, b, 2 * width :].astype(jnp.int32).astype(jnp.float32)
            step = jnp.exp2(mark * (1.0 / LEVELS))[:1] * (scale / (CODE * CODE))
            code = c_ref[y, b, : 2 * width].astype(jnp.int32).astype(jnp.float32)
            total = total + code * jnp.abs(code) * step
        o_ref[0, b] = total[:width]
        o_ref[1, b] = total[width:]


def total_of(codes, scale):
    blocks, nbin, height, _ = codes.shape
    width = (height - 16) // 2
    return pl.pallas_call(
        functools.partial(total_kernel, scale),
        grid=(nbin // 4,),
        in_specs=[pl.BlockSpec((blocks, 4, height, HOP), lambda i: (0, i, 0, 0))],
        out_specs=pl.BlockSpec((2, 4, width, HOP), lambda i: (0, i, 0, 0)),
        out_shape=jax.ShapeDtypeStruct((2, nbin, width, HOP), jnp.float32),
        compiler_params=pltpu.CompilerParams(vmem_limit_bytes=32 * 2**20),
        cost_estimate=pl.CostEstimate(
            flops=6 * blocks * nbin * height * HOP,
            bytes_accessed=3 * blocks * nbin * height * HOP,
            transcendentals=0,
        ),
        name="total",
    )(codes)


def body(samples, taps, bins):
    width, span = samples.shape
    times, chans = lax.axis_size("tm"), lax.axis_size("chan")
    before = passed_along(samples[:, span - SEG :], "tm", 1)
    own = spectra(samples, before, tap_basis(taps, bins))
    mine = lax.all_to_all(own, "chan", 0, 0)
    other = lax.ppermute(mine, "tm", [(i, i ^ 1) for i in range(times)])
    core = (lax.axis_index("tm") % 2).astype(jnp.int32).reshape(1)
    codes = csm_codes(core, mine, other, times // 2)
    height = codes.shape[2]
    same_core = [[t * chans + c for t in range(h, times, 2) for c in range(chans)] for h in range(2)]
    codes = lax.all_to_all(
        codes.reshape(times // 2 * chans, height, HOP),
        ("tm", "chan"),
        0,
        0,
        axis_index_groups=same_core,
    )
    scale = 1.0 / (times * (span // HOP) * 3.0 * SEG / 8.0)
    return total_of(codes.reshape(times // 2, chans, height, HOP), scale)


def solution(mesh):
    return jax.shard_map(
        body,
        mesh=mesh,
        in_specs=(P("chan", "tm"), P("chan", None), P()),
        out_specs=P(None, None, "chan", "tm"),
        check_vma=False,
    )
```

time: 158 us -> 114 us (0.72)
  waiting for transfers between devices: 51.6 us -> 3.92 us
  blocking collectives: 61.1 us -> 79 us
  between operations: 13.7 us -> 0.07 us
  Pallas kernels: 17.3 us -> 26.4 us
  local copies, waits for them, and re-layouts: 8.8 us -> 1.78 us
  matrix products: 2.69 us -> 0 us
    reduce_scatter x1 -> x0, waiting for transfers between devices: 51.6 us -> none  [body(): summed = lax.psum_scatter(partial, 'tm', scatter_dimension=0)]
    all_to_all x1, blocking collectives: 23.5 us -> 41.4 us  [body(): lax.all_to_all(codes.reshape(times // 2 * chans, height, HOP), ('tm', 'ch...]
    pallas_call x1 -> x3, Pallas kernels: 6.57 us -> 15.6 us  [the longest x1 9.98 us: csm_codes(): pl.pallas_call(csm_kernel, in_specs=[pl.BlockSpec(memory_space=pltpu.SMEM...]
    another operation x34 -> x0, local copies, waits for them, and re-layouts: 4.67 us -> none  [tap_basis(): shifted = jnp.stack([ext[:, k:k + 3 * HOP] for k in range(ntap)])]
    ppermute x0 -> x1, waiting for transfers between devices: none -> 3.92 us  [body(): other = lax.ppermute(mine, 'tm', [(i, i ^ 1) for i in range(times)])]
    dot_general x1 -> x0, matrix products: 2.69 us -> none  [tap_basis(): jnp.einsum('ck,krq->crq', taps, shifted, precision=lax.Precision.HIGHEST)]
    dot_general x1 -> x0, local copies, waits for them, and re-layouts: 1.82 us -> none  [tap_basis(): jnp.einsum('ck,krq->crq', taps, shifted, precision=lax.Precision.HIGHEST)]
  transfers between devices with their start and end apart: 2 -> 2, of which waited for: 1 -> 1; matrix products, arithmetic and copies ran while one was open for 7% -> 2% of each run, Pallas kernels for 0% -> 3%
where the time goes in v2:
time: 114 us
  blocking collectives  79 us (69%)
  Pallas kernels  26.4 us (23%)
  waiting for transfers between devices  3.92 us (3%)
  local copies, waits for them, and re-layouts  1.78 us (2%)
  starting transfers between devices  1.66 us (1%)
    all_to_all x1, blocking collectives, body(): lax.all_to_all(codes.reshape(times // 2 * chans, height, HOP), ('tm', 'ch...  41.4 us
    all_to_all x1, blocking collectives, body(): mine = lax.all_to_all(own, 'chan', 0, 0)  37.6 us
    pallas_call x1, Pallas kernels, spectra(): pl.pallas_call(spectra_kernel, grid=(width // 16,), in_specs=[pl.BlockSpe...  10.8 us
    pallas_call x1, Pallas kernels, csm_codes(): pl.pallas_call(csm_kernel, in_specs=[pl.BlockSpec(memory_space=pltpu.SMEM...  9.98 us
    ppermute x1, waiting for transfers between devices, body(): other = lax.ppermute(mine, 'tm', [(i, i ^ 1) for i in range(times)])  3.92 us
    pallas_call x1, Pallas kernels, tap_basis(): pl.pallas_call(weights_kernel, out_shape=jax.ShapeDtypeStruct((3, width *...  3.38 us
  transfers between devices with their start and end apart: 2, of which 1 were waited for; matrix products, arithmetic and copies ran while one was open for 2% of the time, Pallas kernels for 3%

profile of v2, /device:TPU:0, one launch (start us, length us, event | category | flops | bytes accessed | tf_op | source)
XLA Modules:
  0.0 113.7 jit_solution(3491174624155881996)
XLA Ops:
  0.0 0.8 slice.3
  0.8 1.3 %collective-permute-start = (f32[64,256]{1,0:T(8,128)S(1)}, f32[64,256]{1,0:T(8,128)S(1)}, u32[]{:S(2)}, u32[]{:S(2)}) collective-permute-start(f32[64,256]{1,0:T(8,128)S(1)} %slice.3), channel_id=1, source_target_pairs={{0,16},{16,32},{32,48},{48,64},{64,80},{80,96},{96,112},{1,17},{17... | collective-permute-start | bytes 196616 | tf_op jit(solution)/shard_map/ppermute | solution.py:20
  2.2 0.8 cosine_multiply_fusion
  3.1 0.8 copy.5
  3.9 0.1 rev.3.t_ref
  4.0 3.4 %weights.1.v_ref = f32[3,2048,128]{2,1,0:T(8,128)S(1)} custom-call(f32[64,32]{1,0:T(8,128)S(1)} %rev.3.t_ref, f32[32,512]{1,0:T(8,128)S(1)} %pad.4.b_ref), custom_call_target="tpu_custom_call" | custom-call | flops 150994944 | bytes 3145728 | tf_op jit(solution)/shard_map/weights/pallas_call | solution.py:54
  7.3 0.0 collective-permute-done
  7.4 10.8 %spectra.1 = bf16[16,64,1024]{2,1,0:T(8,128)(2,1)S(1)} custom-call(f32[8,4096,128]{2,1,0:T(8,128)} %bitcast.15, f32[8,16,128]{2,1,0:T(8,128)S(1)} %bitcast.14, f32[3,2048,128]{2,1,0:T(8,128)S(1)} %weights.1.v_ref), custom_call_target="tpu_custom_call" | custom-call | flops 3221225472 | bytes 16777216 | tf_op jit(solution)/shard_map/spectra/pallas_call | solution.py:117
  18.2 37.6 %all_to_all.10.own_ref = bf16[16,64,1024]{2,1,0:T(8,128)(2,1)S(1)} all-to-all(bf16[16,64,1024]{2,1,0:T(8,128)(2,1)S(1)} %spectra.1), channel_id=1, replica_groups=mesh['tm'=8,'chan'=16] {'chan'}, dimensions={0} | all-to-all | bytes 4194304 | tf_op jit(solution)/shard_map/all_to_all | solution.py:243
  55.8 0.4 collective-permute-start.1
  56.2 3.9 %collective-permute-done.1.other_ref = bf16[16,64,1024]{2,1,0:T(8,128)(2,1)} collective-permute-done((bf16[16,64,1024]{2,1,0:T(8,128)(2,1)S(1)}, bf16[16,64,1024]{2,1,0:T(8,128)(2,1)}, u32[]{:S(2)}, u32[]{:S(2)}) %collective-permute-start.1) | collective-permute-done | bytes 2097184 | tf_op jit(solution)/shard_map/ppermute | solution.py:244
  60.1 10.0 %csm.1 = s16[4,16,144,128]{3,2,1,0:T(8,128)(2,1)} custom-call(s32[1]{0:T(128)} %bitcast.core_ref, bf16[16,64,1024]{2,1,0:T(8,128)(2,1)S(1)} %all_to_all.10.own_ref, bf16[16,64,1024]{2,1,0:T(8,128)(2,1)} %collective-permute-done.1.other_ref), custom_call_target="tpu_custom_call" | custom-call | flops 4294967296 | bytes 6291456 | tf_op jit(solution)/shard_map/csm/pallas_call | solution.py:185
  70.1 41.4 %all_to_all.11 = s16[64,144,128]{2,1,0:T(8,128)(2,1)S(1)} all-to-all(s16[64,144,128]{2,1,0:T(8,128)(2,1)} %bitcast.16), channel_id=1, replica_groups={{0,1,2,3,4,5,6,7,8,9,10,11,12,13,14,15,32,33,34,35,36,37,38,39,40,41,42..., dimensions={0} | all-to-all | bytes 4718592 | tf_op jit(solution)/shard_map/all_to_all | solution.py:249
  111.5 2.2 %total.1 = f32[2,16,64,128]{3,2,1,0:T(8,128)} custom-call(s16[4,16,144,128]{3,2,1,0:T(8,128)(2,1)S(1)} %bitcast.13), custom_call_target="tpu_custom_call" | custom-call | flops 7077888 | bytes 3538944 | tf_op jit(solution)/shard_map/total/pallas_call | solution.py:222
  (5 shorter events, 0.1 us)
Async XLA Ops:
  0.8 6.5 %collective-permute-start = (f32[64,256]{1,0:T(8,128)S(1)}, f32[64,256]{1,0:T(8,128)S(1)}, u32[]{:S(2)}, u32[]{:S(2)}) collective-permute-start(f32[64,256]{1,0:T(8,128)S(1)} %slice.3), channel_id=1, source_target_pairs={{0,16},{16,32},{32,48},{48,64},{64,80},{80,96},{96,112},{1,17},{17... | collective-permute-start | bytes 196616 | tf_op jit(solution)/shard_map/ppermute | solution.py:20
  55.8 4.3 %collective-permute-start.1 = (bf16[16,64,1024]{2,1,0:T(8,128)(2,1)S(1)}, bf16[16,64,1024]{2,1,0:T(8,128)(2,1)}, u32[]{:S(2)}, u32[]{:S(2)}) collective-permute-start(bf16[16,64,1024]{2,1,0:T(8,128)(2,1)S(1)} %all_to_all.10.own_ref), channel_id=1, source_target_pairs={{0,16},{16,0},{32,48},{48,32},{64,80},{80,64},{96,112},{112,96},{1... | collective-permute-start | bytes 6291464 | tf_op jit(solution)/shard_map/ppermute | solution.py:244

commit v3 on v2

v3 whole, which is shorter than its diff:
```python
import functools
import math

import jax
import jax.numpy as jnp
from jax import lax
from jax.experimental import pallas as pl
from jax.experimental.pallas import tpu as pltpu
from jax.sharding import PartitionSpec as P

SEG = 256
HOP = 128
LEAST = 2.0**-64
STEPS = 312.0
NT = (((1,), (1,)), ((), ()))


def passed_along(block, axis, distance):
    devices = range(lax.axis_size(axis))
    route = [(i - distance, i) for i in devices if i - distance in devices]
    return lax.ppermute(block, axis, route)


def weights_kernel(bins_ref, t_ref, o_ref, b_ref):
    nbin = bins_ref.shape[1]
    nrow, size = b_ref.shape
    ntap, width = t_ref.shape
    index = lax.broadcasted_iota(jnp.int32, (nrow, SEG), 1)
    odd = lax.broadcasted_iota(jnp.int32, (nrow, SEG), 0) % 2
    own_bin = lax.broadcasted_iota(jnp.int32, (nrow, nbin), 0) // 2
    own_bin = own_bin == lax.broadcasted_iota(jnp.int32, (nrow, nbin), 1)
    bins = jnp.where(own_bin, bins_ref[...].astype(jnp.float32), 0.0)
    bins = jnp.sum(bins, axis=1, keepdims=True).astype(jnp.int32)
    window = 0.5 - 0.5 * jnp.cos(2.0 * jnp.pi * index.astype(jnp.float32) / SEG)
    phase = 2.0 * jnp.pi * ((bins * index) & (SEG - 1)).astype(jnp.float32) / SEG
    wave = jnp.where(odd == 0, jnp.cos(phase), -jnp.sin(phase))
    b_ref[:, :HOP] = jnp.zeros((nrow, HOP), jnp.float32)
    b_ref[:, HOP : HOP + SEG] = window * wave
    b_ref[:, HOP + SEG :] = jnp.zeros((nrow, HOP), jnp.float32)
    turn = lax.broadcasted_iota(jnp.int32, (ntap, ntap), 0)
    turn = turn + lax.broadcasted_iota(jnp.int32, (ntap, ntap), 1) == ntap - 1
    turn = jnp.where(turn, 1.0, 0.0).astype(jnp.bfloat16)
    th, tl = split(t_ref[...].T)
    th = jnp.dot(th, turn, preferred_element_type=jnp.float32).astype(jnp.bfloat16)
    tl = jnp.dot(tl, turn, preferred_element_type=jnp.float32).astype(jnp.bfloat16)
    lhs = jnp.concatenate([th, tl, th], axis=1)
    for row in range(nrow):
        line = jnp.broadcast_to(b_ref[row : row + 1, :], (ntap, size))
        line = pltpu.roll(line, size - ntap + 1, 1, stride=1, stride_axis=0)
        high, low = split(line[:, : 3 * HOP])
        rhs = jnp.concatenate([high, high, low], axis=0)
        out = jnp.dot(lhs, rhs, preferred_element_type=jnp.float32)
        for g in range(3):
            o_ref[g * nrow + row] = out[:, g * HOP : (g + 1) * HOP]


def tap_basis(taps, bins):
    width, ntap = taps.shape
    nrow = 2 * bins.shape[0]
    return pl.pallas_call(
        weights_kernel,
        out_shape=jax.ShapeDtypeStruct((3 * nrow, width, HOP), jnp.float32),
        scratch_shapes=[pltpu.VMEM((nrow, 4 * HOP), jnp.float32)],
        compiler_params=pltpu.CompilerParams(vmem_limit_bytes=32 * 2**20),
        cost_estimate=pl.CostEstimate(
            flops=18 * ntap * nrow * width * HOP,
            bytes_accessed=12 * width * nrow * HOP,
            transcendentals=0,
        ),
        name="weights",
    )(bins.reshape(1, -1), taps.T)


def split(value):
    high = value.astype(jnp.bfloat16)
    return high, (value - high.astype(jnp.float32)).astype(jnp.bfloat16)


def spectra_kernel(x_ref, h_ref, v_ref, o_ref, s_ref):
    nrow = 2 * o_ref.shape[0]
    nseg = o_ref.shape[2] // 2
    lines = v_ref.reshape(3 * nrow * 16, HOP)
    lane = lax.broadcasted_iota(jnp.int32, (nrow, nseg), 1)
    for c in range(16):
        g, r = divmod(c, 8)
        x = x_ref[g, pl.ds(r, nseg, stride=8), :]
        data = jnp.concatenate(split(x), axis=1)
        v = lines[pl.ds(c, 3 * nrow, stride=16), :]
        high, low = split(v)
        weights = jnp.concatenate(
            [
                jnp.concatenate([high, high], axis=1),
                jnp.concatenate([low, jnp.zeros_like(low)], axis=1),
            ],
            axis=0,
        )
        z = lax.dot_general(weights, data, NT, preferred_element_type=jnp.float32)
        z = z[: 3 * nrow] + z[3 * nrow :]
        older = h_ref[g, r : r + 1, :]
        newer = h_ref[g, 8 + r : 9 + r, :]
        first = jnp.sum(v[nrow : 2 * nrow] * newer + v[:nrow] * older, axis=1, keepdims=True)
        second = jnp.sum(v[:nrow] * newer, axis=1, keepdims=True)
        z1 = jnp.where(lane == 0, first, pltpu.roll(z[nrow : 2 * nrow], 1, 1))
        z0 = jnp.where(lane == 1, second, pltpu.roll(z[:nrow], 2, 1))
        z0 = jnp.where(lane == 0, 0.0, z0)
        total = z[2 * nrow :] + z1 + z0
        for i in range(nseg // 128):
            s_ref[i, pl.ds(c, nrow, stride=16), :] = total[:, i * 128 : (i + 1) * 128]
    for j in range(nrow):
        for i in range(nseg // 128):
            part = s_ref[i, j * 16 : (j + 1) * 16, :]
            at = j % 2 * nseg + i * 128
            o_ref[j // 2, :, at : at + 128] = part.astype(jnp.bfloat16)


def spectra(samples, before, weights):
    width, span = samples.shape
    nseg = span // HOP
    nrow = weights.shape[0] // 3

    def by_rows(a):
        n = a.shape[1] // HOP
        return a.reshape(width // 8, 8, n, HOP).transpose(0, 2, 1, 3).reshape(width // 8, n * 8, HOP)

    return pl.pallas_call(
        spectra_kernel,
        grid=(width // 16,),
        in_specs=[
            pl.BlockSpec((2, nseg * 8, HOP), lambda i: (i, 0, 0)),
            pl.BlockSpec((2, 16, HOP), lambda i: (i, 0, 0)),
            pl.BlockSpec((3 * nrow, 16, HOP), lambda i: (0, i, 0)),
        ],
        out_specs=pl.BlockSpec((nrow // 2, 16, 2 * nseg), lambda i: (0, i, 0)),
        out_shape=jax.ShapeDtypeStruct((nrow // 2, width, 2 * nseg), jnp.bfloat16),
        scratch_shapes=[pltpu.VMEM((nseg // 128, nrow * 16, 128), jnp.float32)],
        compiler_params=pltpu.CompilerParams(vmem_limit_bytes=48 * 2**20),
        cost_estimate=pl.CostEstimate(
            flops=2 * 2 * 6 * nrow * width * span, bytes_accessed=width * span * 4, transcendentals=0
        ),
        name="spectra",
    )(by_rows(samples), by_rows(before), weights)


def columns_of(ref, at):
    _, width, depth = ref.shape
    nseg = depth // 2
    cols = ref[pl.ds(at, HOP // width)].reshape(HOP, depth)
    turned = jnp.concatenate([-cols[:, nseg:], cols[:, :nseg]], axis=1)
    return jnp.concatenate([cols, turned], axis=0)


def product(ref, r, columns):
    _, width, depth = ref.shape
    rows = ref[r : r + 4].reshape(4 * width, depth)
    return lax.dot_general(rows, columns, NT, preferred_element_type=jnp.float32)


def own_kernel(core_ref, own_ref, p_ref):
    nsrc, width, _ = own_ref.shape
    core = core_ref[0]
    for y in range(p_ref.shape[0]):
        own = columns_of(own_ref, (2 * y + core) * (HOP // width))
        for r in range(0, nsrc, 4):
            p_ref[y, r * width : (r + 4) * width, :] = product(own_ref, r, own)


def code_kernel(core_ref, other_ref, p_ref, o_ref):
    nsrc, width, _ = other_ref.shape
    core = core_ref[0]
    for y in range(p_ref.shape[0]):
        other = columns_of(other_ref, (2 * y + core) * (HOP // width))
        for r in range(0, nsrc, 4):
            part = product(other_ref, r, other) + p_ref[y, r * width : (r + 4) * width, :]
            level = jnp.log2(jnp.maximum(jnp.abs(part), LEAST))
            code = (level * STEPS + (0.5 - math.log2(LEAST) * STEPS)).astype(jnp.int32)
            code = jnp.where(part < 0.0, -code, code).astype(jnp.int16)
            code = code.reshape(4, width, 2 * HOP)
            o_ref[y, r : r + 4, :width] = code[:, :, :HOP]
            o_ref[y, r : r + 4, width:] = code[:, :, HOP:]


def own_products(core, own, blocks):
    nsrc, width, depth = own.shape
    chans = nsrc * width
    return pl.pallas_call(
        own_kernel,
        in_specs=[
            pl.BlockSpec(memory_space=pltpu.SMEM),
            pl.BlockSpec(memory_space=pltpu.VMEM),
        ],
        out_specs=pl.BlockSpec(memory_space=pltpu.VMEM),
        out_shape=jax.ShapeDtypeStruct((blocks, chans, 2 * HOP), jnp.float32),
        compiler_params=pltpu.CompilerParams(vmem_limit_bytes=24 * 2**20),
        cost_estimate=pl.CostEstimate(
            flops=4 * chans * blocks * HOP * depth,
            bytes_accessed=2 * chans * (depth + 4 * blocks * HOP),
            transcendentals=0,
        ),
        name="own_products",
    )(core, own)


def product_codes(core, other, partial):
    nsrc, width, depth = other.shape
    blocks, chans, _ = partial.shape
    return pl.pallas_call(
        code_kernel,
        in_specs=[
            pl.BlockSpec(memory_space=pltpu.SMEM),
            pl.BlockSpec(memory_space=pltpu.VMEM),
            pl.BlockSpec(memory_space=pltpu.VMEM),
        ],
        out_specs=pl.BlockSpec(memory_space=pltpu.VMEM),
        out_shape=jax.ShapeDtypeStruct((blocks, nsrc, 2 * width, HOP), jnp.int16),
        compiler_params=pltpu.CompilerParams(vmem_limit_bytes=32 * 2**20),
        cost_estimate=pl.CostEstimate(
            flops=4 * chans * blocks * HOP * depth,
            bytes_accessed=2 * chans * (depth + 6 * blocks * HOP),
            transcendentals=chans * blocks * HOP * 2,
        ),
        name="product_codes",
    )(core, other, partial)


def total_kernel(scale, c_ref, o_ref):
    blocks, nbin, _, _ = c_ref.shape
    width = o_ref.shape[2]
    for b in range(nbin):
        total = jnp.zeros((2 * width, HOP), jnp.float32)
        for y in range(blocks):
            code = c_ref[y, b].astype(jnp.int32).astype(jnp.float32)
            level = jnp.abs(code) * (1.0 / STEPS) + math.log2(LEAST * scale)
            size = jnp.exp2(level)
            total = total + jnp.where(code > 0.0, size, jnp.where(code < 0.0, -size, 0.0))
        o_ref[0, b] = total[:width]
        o_ref[1, b] = total[width:]


def total_of(codes, scale):
    blocks, nbin, height, _ = codes.shape
    width = height // 2
    return pl.pallas_call(
        functools.partial(total_kernel, scale),
        grid=(nbin // 4,),
        in_specs=[pl.BlockSpec((blocks, 4, height, HOP), lambda i: (0, i, 0, 0))],
        out_specs=pl.BlockSpec((2, 4, width, HOP), lambda i: (0, i, 0, 0)),
        out_shape=jax.ShapeDtypeStruct((2, nbin, width, HOP), jnp.float32),
        compiler_params=pltpu.CompilerParams(vmem_limit_bytes=32 * 2**20),
        cost_estimate=pl.CostEstimate(
            flops=6 * blocks * nbin * height * HOP,
            bytes_accessed=3 * blocks * nbin * height * HOP,
            transcendentals=blocks * nbin * height * HOP,
        ),
        name="total",
    )(codes)


def body(samples, taps, bins):
    width, span = samples.shape
    times, chans = lax.axis_size("tm"), lax.axis_size("chan")
    before = passed_along(samples[:, span - SEG :], "tm", 1)
    own = spectra(samples, before, tap_basis(taps, bins))
    mine = lax.all_to_all(own, "chan", 0, 0)
    other = lax.ppermute(mine, "tm", [(i, i ^ 1) for i in range(times)])
    core = (lax.axis_index("tm") % 2).astype(jnp.int32).reshape(1)
    codes = product_codes(core, other, own_products(core, mine, times // 2))
    height = codes.shape[2]
    same_core = [[t * chans + c for t in range(h, times, 2) for c in range(chans)] for h in range(2)]
    codes = lax.all_to_all(
        codes.reshape(times // 2 * chans, height, HOP),
        ("tm", "chan"),
        0,
        0,
        axis_index_groups=same_core,
    )
    scale = 1.0 / (times * (span // HOP) * 3.0 * SEG / 8.0)
    return total_of(codes.reshape(times // 2, chans, height, HOP), scale)


def solution(mesh):
    return jax.shard_map(
        body,
        mesh=mesh,
        in_specs=(P("chan", "tm"), P("chan", None), P()),
        out_specs=P(None, None, "chan", "tm"),
        check_vma=False,
    )
```

time: 114 us -> 104 us (0.912)
  Pallas kernels: 26.4 us -> 22.7 us
  blocking collectives: 79 us -> 75.7 us
  waiting for transfers between devices: 3.92 us -> 1.55 us
    pallas_call x2 -> x3, Pallas kernels: 13.4 us -> 8.72 us  [the longest x1 5.33 us: product_codes(): pl.pallas_call(code_kernel, in_specs=[pl.BlockSpec(memory_space=pltpu.SME...]
    all_to_all x1, blocking collectives: 41.4 us -> 38.1 us  [body(): lax.all_to_all(codes.reshape(times // 2 * chans, height, HOP), ('tm', 'ch...]
    ppermute x1, waiting for transfers between devices: 3.92 us -> 1.54 us  [body(): other = lax.ppermute(mine, 'tm', [(i, i ^ 1) for i in range(times)])]
  transfers between devices with their start and end apart: 2 -> 2, of which waited for: 1 -> 1; matrix products, arithmetic and copies ran while one was open for 2% -> 0% of each run, Pallas kernels for 3% -> 3%
where the time goes in v3:
time: 104 us
  blocking collectives  75.7 us (73%)
  Pallas kernels  22.7 us (22%)
  local copies, waits for them, and re-layouts  2.21 us (2%)
  starting transfers between devices  1.66 us (2%)
  waiting for transfers between devices  1.55 us (1%)
    all_to_all x1, blocking collectives, body(): lax.all_to_all(codes.reshape(times // 2 * chans, height, HOP), ('tm', 'ch...  38.1 us
    all_to_all x1, blocking collectives, body(): mine = lax.all_to_all(own, 'chan', 0, 0)  37.6 us
    pallas_call x1, Pallas kernels, spectra(): pl.pallas_call(spectra_kernel, grid=(width // 16,), in_specs=[pl.BlockSpe...  11.3 us
    pallas_call x1, Pallas kernels, product_codes(): pl.pallas_call(code_kernel, in_specs=[pl.BlockSpec(memory_space=pltpu.SME...  5.33 us
    pallas_call x1, Pallas kernels, total_of(): pl.pallas_call(functools.partial(total_kernel, scale), grid=(nbin // 4,),...  2.76 us
    pallas_call x1, Pallas kernels, own_products(): pl.pallas_call(own_kernel, in_specs=[pl.BlockSpec(memory_space=pltpu.SMEM...  2.37 us
  transfers between devices with their start and end apart: 2, of which 1 were waited for; matrix products, arithmetic and copies ran while one was open for 0% of the time, Pallas kernels for 3%

profile of v3, /device:TPU:0, one launch (start us, length us, event | category | flops | bytes accessed | tf_op | source)
XLA Modules:
  0.0 103.9 jit_solution(3993714626527803842)
XLA Ops:
  0.0 0.8 slice.3
  0.8 1.3 %collective-permute-start = (f32[64,256]{1,0:T(8,128)S(1)}, f32[64,256]{1,0:T(8,128)S(1)}, u32[]{:S(2)}, u32[]{:S(2)}) collective-permute-start(f32[64,256]{1,0:T(8,128)S(1)} %slice.3), channel_id=1, source_target_pairs={{0,16},{16,32},{32,48},{48,64},{64,80},{80,96},{96,112},{1,17},{17... | collective-permute-start | bytes 196616 | tf_op jit(solution)/shard_map/ppermute | solution.py:21
  2.1 0.0 copy-start
  2.1 0.7 copy-done
  2.9 0.0 copy-start.1
  2.9 0.7 copy-done.1
  3.5 1.0 weights.1.v_ref
  4.5 0.0 collective-permute-done
  4.5 11.3 %spectra.1 = bf16[16,64,1024]{2,1,0:T(8,128)(2,1)S(1)} custom-call(f32[8,4096,128]{2,1,0:T(8,128)} %bitcast.20, f32[8,16,128]{2,1,0:T(8,128)S(1)} %bitcast.17, f32[96,64,128]{2,1,0:T(8,128)S(1)} %weights.1.v_ref), custom_call_target="tpu_custom_call" | custom-call | flops 3221225472 | bytes 16777216 | tf_op jit(solution)/shard_map/spectra/pallas_call | solution.py:125
  15.8 37.6 %all_to_all.10.own_ref = bf16[16,64,1024]{2,1,0:T(8,128)(2,1)S(1)} all-to-all(bf16[16,64,1024]{2,1,0:T(8,128)(2,1)S(1)} %spectra.1), channel_id=1, replica_groups=mesh['tm'=8,'chan'=16] {'chan'}, dimensions={0} | all-to-all | bytes 4194304 | tf_op jit(solution)/shard_map/all_to_all | solution.py:263
  53.4 0.4 collective-permute-start.1
  53.8 2.4 %own_products.1.p_ref = f32[4,1024,256]{2,1,0:T(8,128)S(1)} custom-call(s32[1]{0:T(128)} %bitcast.core_ref, bf16[16,64,1024]{2,1,0:T(8,128)(2,1)S(1)} %all_to_all.10.own_ref), custom_call_target="tpu_custom_call" | custom-call | flops 2147483648 | bytes 6291456 | tf_op jit(solution)/shard_map/own_products/pallas_call | solution.py:185
  56.2 1.5 %collective-permute-done.1.other_ref = bf16[16,64,1024]{2,1,0:T(8,128)(2,1)} collective-permute-done((bf16[16,64,1024]{2,1,0:T(8,128)(2,1)S(1)}, bf16[16,64,1024]{2,1,0:T(8,128)(2,1)}, u32[]{:S(2)}, u32[]{:S(2)}) %collective-permute-start.1) | collective-permute-done | bytes 2097184 | tf_op jit(solution)/shard_map/ppermute | solution.py:264
  57.7 5.3 %product_codes.1 = s16[4,16,128,128]{3,2,1,0:T(8,128)(2,1)S(1)} custom-call(s32[1]{0:T(128)} %bitcast.core_ref, bf16[16,64,1024]{2,1,0:T(8,128)(2,1)} %collective-permute-done.1.other_ref, f32[4,1024,256]{2,1,0:T(8,128)S(1)} %own_products.1.p_ref), custom_call_target="tpu_custom_call" | custom-call | flops 2147483648 | bytes 8388608 | tf_op jit(solution)/shard_map/product_codes/pallas_call | solution.py:206
  63.0 38.1 %all_to_all.11 = s16[64,128,128]{2,1,0:T(8,128)(2,1)S(1)} all-to-all(s16[64,128,128]{2,1,0:T(8,128)(2,1)S(1)} %bitcast.16), channel_id=1, replica_groups={{0,1,2,3,4,5,6,7,8,9,10,11,12,13,14,15,32,33,34,35,36,37,38,39,40,41,42..., dimensions={0} | all-to-all | bytes 4194304 | tf_op jit(solution)/shard_map/all_to_all | solution.py:269
  101.1 2.8 %total.1 = f32[2,16,64,128]{3,2,1,0:T(8,128)} custom-call(s16[4,16,128,128]{3,2,1,0:T(8,128)(2,1)S(1)} %bitcast.15), custom_call_target="tpu_custom_call" | custom-call | flops 6291456 | bytes 3145728 | tf_op jit(solution)/shard_map/total/pallas_call | solution.py:242
Async XLA Ops:
  0.8 3.7 %collective-permute-start = (f32[64,256]{1,0:T(8,128)S(1)}, f32[64,256]{1,0:T(8,128)S(1)}, u32[]{:S(2)}, u32[]{:S(2)}) collective-permute-start(f32[64,256]{1,0:T(8,128)S(1)} %slice.3), channel_id=1, source_target_pairs={{0,16},{16,32},{32,48},{48,64},{64,80},{80,96},{96,112},{1,17},{17... | collective-permute-start | bytes 196616 | tf_op jit(solution)/shard_map/ppermute | solution.py:21
  2.1 0.7 copy-start
  2.9 0.7 copy-start.1
  53.4 4.3 %collective-permute-start.1 = (bf16[16,64,1024]{2,1,0:T(8,128)(2,1)S(1)}, bf16[16,64,1024]{2,1,0:T(8,128)(2,1)}, u32[]{:S(2)}, u32[]{:S(2)}) collective-permute-start(bf16[16,64,1024]{2,1,0:T(8,128)(2,1)S(1)} %all_to_all.10.own_ref), channel_id=1, source_target_pairs={{0,16},{16,0},{32,48},{48,32},{64,80},{80,64},{96,112},{112,96},{1... | collective-permute-start | bytes 6291464 | tf_op jit(solution)/shard_map/ppermute | solution.py:264

commit v4 on v3

v4 whole, which is shorter than its diff:
```python
import functools
import math

import jax
import jax.numpy as jnp
from jax import lax
from jax.experimental import pallas as pl
from jax.experimental.pallas import tpu as pltpu
from jax.sharding import PartitionSpec as P

SEG = 256
HOP = 128
LEAST = 2.0**-64
STEPS = 312.0
NT = (((1,), (1,)), ((), ()))


def passed_along(block, axis, distance):
    devices = range(lax.axis_size(axis))
    route = [(i - distance, i) for i in devices if i - distance in devices]
    return lax.ppermute(block, axis, route)


def split(value):
    high = value.astype(jnp.bfloat16)
    return high, (value - high.astype(jnp.float32)).astype(jnp.bfloat16)


def fill_weights(t_ref, b_ref, v_ref):
    nrow, size = b_ref.shape
    nbin = nrow // 2
    ntap, width = t_ref.shape[0] - 8, t_ref.shape[1]
    index = lax.broadcasted_iota(jnp.int32, (nrow, SEG), 1)
    odd = lax.broadcasted_iota(jnp.int32, (nrow, SEG), 0) % 2
    own_bin = lax.broadcasted_iota(jnp.int32, (nrow, nbin), 0) // 2
    own_bin = own_bin == lax.broadcasted_iota(jnp.int32, (nrow, nbin), 1)
    bins = jnp.where(own_bin, t_ref[ntap : ntap + 1, :nbin], 0.0)
    bins = jnp.sum(bins, axis=1, keepdims=True).astype(jnp.int32)
    window = 0.5 - 0.5 * jnp.cos(2.0 * jnp.pi * index.astype(jnp.float32) / SEG)
    phase = 2.0 * jnp.pi * ((bins * index) & (SEG - 1)).astype(jnp.float32) / SEG
    wave = jnp.where(odd == 0, jnp.cos(phase), -jnp.sin(phase))
    b_ref[:, :HOP] = jnp.zeros((nrow, HOP), jnp.float32)
    b_ref[:, HOP : HOP + SEG] = window * wave
    b_ref[:, HOP + SEG :] = jnp.zeros((nrow, HOP), jnp.float32)
    turn = lax.broadcasted_iota(jnp.int32, (ntap, ntap), 0)
    turn = turn + lax.broadcasted_iota(jnp.int32, (ntap, ntap), 1) == ntap - 1
    turn = jnp.where(turn, 1.0, 0.0).astype(jnp.bfloat16)
    th, tl = split(t_ref[:ntap].T)
    th = jnp.dot(th, turn, preferred_element_type=jnp.float32).astype(jnp.bfloat16)
    tl = jnp.dot(tl, turn, preferred_element_type=jnp.float32).astype(jnp.bfloat16)
    lhs = jnp.concatenate([th, tl, th], axis=1)
    for row in range(nrow):
        line = jnp.broadcast_to(b_ref[row : row + 1, :], (ntap, size))
        line = pltpu.roll(line, size - ntap + 1, 1, stride=1, stride_axis=0)
        high, low = split(line[:, : 3 * HOP])
        rhs = jnp.concatenate([high, high, low], axis=0)
        out = jnp.dot(lhs, rhs, preferred_element_type=jnp.float32)
        for g in range(3):
            for i in range(width // 16):
                at = ((i * 3 + g) * nrow + row) * 16
                part = out[i * 16 : (i + 1) * 16, g * HOP : (g + 1) * HOP]
                v_ref[at : at + 16, :] = part


def taps_and_bins(taps, bins):
    width, ntap = taps.shape
    below = lax.broadcasted_iota(jnp.int32, (ntap + 8, width), 0) >= ntap
    bins = jnp.pad(bins.astype(jnp.float32), (0, width - bins.shape[0]))
    return jnp.where(below, bins[None, :], jnp.pad(taps.T, ((0, 8), (0, 0))))


def spectra_kernel(t_ref, x_ref, h_ref, o_ref, b_ref, v_ref, x_buf, s_ref, sems):
    nrow = 2 * o_ref.shape[0]
    width = o_ref.shape[1]
    nseg = o_ref.shape[2] // 2
    groups = width // 8
    copies = [
        pltpu.make_async_copy(x_ref.at[g], x_buf.at[g], sems.at[g]) for g in range(groups)
    ]
    waits = {0: copies[:1], 1: copies[1:2], 2: copies[2:4], 4: copies[4:]}
    starts = {1: copies[4:6], 2: copies[6:]}
    for copy in copies[:4]:
        copy.start()
    fill_weights(t_ref, b_ref, v_ref)
    lane = lax.broadcasted_iota(jnp.int32, (nrow, HOP), 1)

    def finish(i, j):
        for k in range(nseg // 128):
            part = s_ref[i % 2, k, j * 16 : (j + 1) * 16, :]
            at = j % 2 * nseg + k * 128
            o_ref[j // 2, i * 16 : (i + 1) * 16, at : at + 128] = part.astype(jnp.bfloat16)

    for c in range(width):
        g, r = divmod(c, 8)
        i, c16 = divmod(c, 16)
        if r == 0:
            for copy in waits.get(g, []):
                copy.wait()
            for copy in starts.get(g, []):
                copy.start()
        x = x_buf[g, pl.ds(r, nseg, stride=8), :]
        data = jnp.concatenate(split(x), axis=1)
        v = v_ref[pl.ds(i * 3 * nrow * 16 + c16, 3 * nrow, stride=16), :]
        high, low = split(v)
        weights = jnp.concatenate(
            [
                jnp.concatenate([high, high], axis=1),
                jnp.concatenate([low, jnp.zeros_like(low)], axis=1),
            ],
            axis=0,
        )
        z = lax.dot_general(weights, data, NT, preferred_element_type=jnp.float32)
        z = z[: 3 * nrow] + z[3 * nrow :]
        older = h_ref[g, r : r + 1, :]
        newer = h_ref[g, 8 + r : 9 + r, :]
        first = jnp.sum(v[nrow : 2 * nrow] * newer + v[:nrow] * older, axis=1, keepdims=True)
        second = jnp.sum(v[:nrow] * newer, axis=1, keepdims=True)
        past = pltpu.roll(z[nrow : 2 * nrow], 1, 1) + pltpu.roll(z[:nrow], 2, 1)
        second = z[nrow : 2 * nrow, :1] + second
        start = jnp.where(lane == 0, first, jnp.where(lane == 1, second, past[:, :HOP]))
        total = z[2 * nrow :] + jnp.concatenate([start, past[:, HOP:]], axis=1)
        for k in range(nseg // 128):
            s_ref[i % 2, k, pl.ds(c16, nrow, stride=16), :] = total[:, k * 128 : (k + 1) * 128]
        if i > 0:
            for j in range(c16 * nrow // 16, (c16 + 1) * nrow // 16):
                finish(i - 1, j)
    for j in range(nrow):
        finish(width // 16 - 1, j)


def spectra(samples, before, taps, bins):
    width, span = samples.shape
    nseg = span // HOP
    nrow = 2 * bins.shape[0]

    def by_rows(a):
        n = a.shape[1] // HOP
        return a.reshape(width // 8, 8, n, HOP).transpose(0, 2, 1, 3).reshape(width // 8, n * 8, HOP)

    return pl.pallas_call(
        spectra_kernel,
        in_specs=[
            pl.BlockSpec(memory_space=pltpu.VMEM),
            pl.BlockSpec(memory_space=pl.ANY),
            pl.BlockSpec(memory_space=pltpu.VMEM),
        ],
        out_specs=pl.BlockSpec(memory_space=pltpu.VMEM),
        out_shape=jax.ShapeDtypeStruct((nrow // 2, width, 2 * nseg), jnp.bfloat16),
        scratch_shapes=[
            pltpu.VMEM((nrow, 4 * HOP), jnp.float32),
            pltpu.VMEM((width * 3 * nrow, HOP), jnp.float32),
            pltpu.VMEM((width // 8, nseg * 8, HOP), jnp.float32),
            pltpu.VMEM((2, nseg // 128, nrow * 16, 128), jnp.float32),
            pltpu.SemaphoreType.DMA((width // 8,)),
        ],
        compiler_params=pltpu.CompilerParams(vmem_limit_bytes=48 * 2**20),
        cost_estimate=pl.CostEstimate(
            flops=2 * 2 * 6 * nrow * width * span, bytes_accessed=width * span * 4, transcendentals=0
        ),
        name="spectra",
    )(taps_and_bins(taps, bins), by_rows(samples), by_rows(before))


def columns_of(ref, y, core):
    _, width, depth = ref.shape
    nseg = depth // 2
    take = HOP // width
    cols = ref[pl.ds((2 * y + core) * take, take)].reshape(HOP, depth)
    turned = jnp.concatenate([-cols[:, nseg:], cols[:, :nseg]], axis=1)
    return jnp.concatenate([cols, turned], axis=0)


def product(ref, r, columns):
    _, width, depth = ref.shape
    rows = ref[r : r + 4].reshape(4 * width, depth)
    return lax.dot_general(rows, columns, NT, preferred_element_type=jnp.float32)


def own_kernel(core_ref, own_hbm, p_ref, own_ref, sems):
    nsrc, width, _ = own_ref.shape
    copies = [pltpu.make_async_copy(own_hbm.at[r], own_ref.at[r], sems.at[r]) for r in range(nsrc)]
    for copy in copies:
        copy.start()
    for copy in copies:
        copy.wait()
    for y in range(p_ref.shape[0]):
        own = columns_of(own_ref, y, core_ref[0])
        for r in range(0, nsrc, 4):
            p_ref[y, r * width : (r + 4) * width, :] = product(own_ref, r, own)


def code_kernel(core_ref, other_ref, columns_ref, p_ref, o_ref):
    nsrc, width, _ = other_ref.shape
    for y in range(p_ref.shape[0]):
        other = columns_of(columns_ref, y, core_ref[0])
        for r in range(0, nsrc, 4):
            part = product(other_ref, r, other) + p_ref[y, r * width : (r + 4) * width, :]
            level = jnp.log2(jnp.maximum(jnp.abs(part), LEAST))
            code = (level * STEPS + (0.5 - math.log2(LEAST) * STEPS)).astype(jnp.int32)
            code = jnp.where(part < 0.0, -code, code).astype(jnp.int16)
            code = code.reshape(4, width, 2 * HOP)
            o_ref[y, r : r + 4, :width] = code[:, :, :HOP]
            o_ref[y, r : r + 4, width:] = code[:, :, HOP:]


def own_products(core, own, blocks):
    nsrc, width, depth = own.shape
    chans = nsrc * width
    return pl.pallas_call(
        own_kernel,
        in_specs=[
            pl.BlockSpec(memory_space=pltpu.SMEM),
            pl.BlockSpec(memory_space=pl.ANY),
        ],
        out_specs=pl.BlockSpec(memory_space=pltpu.VMEM),
        out_shape=jax.ShapeDtypeStruct((blocks, chans, 2 * HOP), jnp.float32),
        scratch_shapes=[
            pltpu.VMEM((nsrc, width, depth), jnp.bfloat16),
            pltpu.SemaphoreType.DMA((nsrc,)),
        ],
        compiler_params=pltpu.CompilerParams(vmem_limit_bytes=24 * 2**20),
        cost_estimate=pl.CostEstimate(
            flops=4 * chans * blocks * HOP * depth,
            bytes_accessed=2 * chans * (depth + 4 * blocks * HOP),
            transcendentals=0,
        ),
        name="own_products",
    )(core, own)


def product_codes(core, other, partial):
    nsrc, width, depth = other.shape
    blocks, chans, _ = partial.shape
    return pl.pallas_call(
        code_kernel,
        in_specs=[
            pl.BlockSpec(memory_space=pltpu.SMEM),
            pl.BlockSpec(memory_space=pltpu.VMEM),
            pl.BlockSpec(memory_space=pltpu.VMEM),
            pl.BlockSpec(memory_space=pltpu.VMEM),
        ],
        out_specs=pl.BlockSpec(memory_space=pltpu.VMEM),
        out_shape=jax.ShapeDtypeStruct((blocks, nsrc, 2 * width, HOP), jnp.int16),
        compiler_params=pltpu.CompilerParams(vmem_limit_bytes=32 * 2**20),
        cost_estimate=pl.CostEstimate(
            flops=4 * chans * blocks * HOP * depth,
            bytes_accessed=2 * chans * (depth + 6 * blocks * HOP),
            transcendentals=chans * blocks * HOP * 2,
        ),
        name="product_codes",
    )(core, other, other, partial)


def total_kernel(scale, c_ref, o_ref, buf, sems):
    blocks, nbin, _, _ = c_ref.shape
    width = buf.shape[2]
    copies = []
    for b in range(nbin):
        total = jnp.zeros((2 * width, HOP), jnp.float32)
        for y in range(blocks):
            code = c_ref[y, b].astype(jnp.int32).astype(jnp.float32)
            level = jnp.abs(code) * (1.0 / STEPS) + math.log2(LEAST * scale)
            size = jnp.exp2(level)
            total = total + jnp.where(code > 0.0, size, jnp.where(code < 0.0, -size, 0.0))
        buf[0, b] = total[:width]
        buf[1, b] = total[width:]
        if b % 2 == 1:
            both = pl.ds(b - 1, 2)
            copy = pltpu.make_async_copy(buf.at[:, both], o_ref.at[:, both], sems.at[b // 2])
            copy.start()
            copies.append(copy)
    for copy in copies:
        copy.wait()


def total_of(codes, scale):
    blocks, nbin, height, _ = codes.shape
    width = height // 2
    return pl.pallas_call(
        functools.partial(total_kernel, scale),
        in_specs=[pl.BlockSpec(memory_space=pltpu.VMEM)],
        out_specs=pl.BlockSpec(memory_space=pltpu.HBM),
        out_shape=jax.ShapeDtypeStruct((2, nbin, width, HOP), jnp.float32),
        scratch_shapes=[
            pltpu.VMEM((2, nbin, width, HOP), jnp.float32),
            pltpu.SemaphoreType.DMA((nbin // 2,)),
        ],
        compiler_params=pltpu.CompilerParams(vmem_limit_bytes=32 * 2**20),
        cost_estimate=pl.CostEstimate(
            flops=6 * blocks * nbin * height * HOP,
            bytes_accessed=3 * blocks * nbin * height * HOP,
            transcendentals=blocks * nbin * height * HOP,
        ),
        name="total",
    )(codes)


def body(samples, taps, bins):
    width, span = samples.shape
    times, chans = lax.axis_size("tm"), lax.axis_size("chan")
    before = passed_along(samples[:, span - SEG :], "tm", 1)
    own = spectra(samples, before, taps, bins)
    mine = lax.all_to_all(own, "chan", 0, 0)
    other = lax.ppermute(mine, "tm", [(i, i ^ 1) for i in range(times)])
    core = (lax.axis_index("tm") % 2).astype(jnp.int32).reshape(1)
    codes = product_codes(core, other, own_products(core, mine, times // 2))
    height = codes.shape[2]
    same_core = [[t * chans + c for t in range(h, times, 2) for c in range(chans)] for h in range(2)]
    codes = lax.all_to_all(
        codes.reshape(times // 2 * chans, height, HOP),
        ("tm", "chan"),
        0,
        0,
        axis_index_groups=same_core,
    )
    scale = 1.0 / (times * (span // HOP) * 3.0 * SEG / 8.0)
    return total_of(codes.reshape(times // 2, chans, height, HOP), scale)


def solution(mesh):
    return jax.shard_map(
        body,
        mesh=mesh,
        in_specs=(P("chan", "tm"), P("chan", None), P()),
        out_specs=P(None, None, "chan", "tm"),
        check_vma=False,
    )
```

time: 104 us -> 102 us (0.981)
  waiting for transfers between devices: 1.55 us -> 0.01 us
  other arithmetic: 0 us -> 1.46 us
  Pallas kernels: 22.7 us -> 21.3 us
  local copies, waits for them, and re-layouts: 2.21 us -> 0.85 us
    pallas_call x1, Pallas kernels: 2.37 us -> 4.1 us  [own_products(): pl.pallas_call(own_kernel, in_specs=[pl.BlockSpec(memory_space=pltpu.SMEM...]
    pallas_call x3 -> x2, Pallas kernels: 15 us -> 13.4 us  [the longest x1 11.1 us: spectra(): pl.pallas_call(spectra_kernel, in_specs=[pl.BlockSpec(memory_space=pltpu....]
    pallas_call x1, Pallas kernels: 5.33 us -> 3.73 us  [product_codes(): pl.pallas_call(code_kernel, in_specs=[pl.BlockSpec(memory_space=pltpu.SME...]
    ppermute x1, waiting for transfers between devices: 1.54 us -> 0.01 us  [body(): other = lax.ppermute(mine, 'tm', [(i, i ^ 1) for i in range(times)])]
    unnamed x4 -> x0, local copies, waits for them, and re-layouts: 1.37 us -> none
  transfers between devices with their start and end apart: 2 -> 2, of which waited for: 1 -> 0; matrix products, arithmetic and copies ran while one was open for 0% -> 1% of each run, Pallas kernels for 3% -> 4%
where the time goes in v4:
time: 102 us; the launch traced here: 101 us
  blocking collectives  76 us (75%)
  Pallas kernels  21.3 us (21%)
  starting transfers between devices  1.66 us (2%)
  other arithmetic  1.46 us (1%)
    all_to_all x1, blocking collectives, body(): lax.all_to_all(codes.reshape(times // 2 * chans, height, HOP), ('tm', 'ch...  38.3 us
    all_to_all x1, blocking collectives, body(): mine = lax.all_to_all(own, 'chan', 0, 0)  37.7 us
    pallas_call x1, Pallas kernels, spectra(): pl.pallas_call(spectra_kernel, in_specs=[pl.BlockSpec(memory_space=pltpu....  11.1 us
    pallas_call x1, Pallas kernels, own_products(): pl.pallas_call(own_kernel, in_specs=[pl.BlockSpec(memory_space=pltpu.SMEM...  4.1 us
    pallas_call x1, Pallas kernels, product_codes(): pl.pallas_call(code_kernel, in_specs=[pl.BlockSpec(memory_space=pltpu.SME...  3.73 us
    pallas_call x1, Pallas kernels, total_of(): pl.pallas_call(functools.partial(total_kernel, scale), in_specs=[pl.Block...  2.32 us
  transfers between devices with their start and end apart: 2, of which 0 were waited for; matrix products, arithmetic and copies ran while one was open for 1% of the time, Pallas kernels for 4%

profile of v4, /device:TPU:0, one launch (start us, length us, event | category | flops | bytes accessed | tf_op | source)
XLA Modules:
  0.0 101.4 jit_solution(4166485288271728789)
XLA Ops:
  0.0 0.8 slice.3
  0.8 1.3 %collective-permute-start = (f32[64,256]{1,0:T(8,128)S(1)}, f32[64,256]{1,0:T(8,128)S(1)}, u32[]{:S(2)}, u32[]{:S(2)}) collective-permute-start(f32[64,256]{1,0:T(8,128)S(1)} %slice.3), channel_id=1, source_target_pairs={{0,16},{16,32},{32,48},{48,64},{64,80},{80,96},{96,112},{1,17},{17... | collective-permute-start | bytes 196616 | tf_op jit(solution)/shard_map/ppermute | solution.py:21
  2.1 0.7 convert_element_type.7
  2.8 0.8 pad_select_fusion.t_ref
  3.6 0.0 collective-permute-done
  3.6 11.1 %spectra.1 = bf16[16,64,1024]{2,1,0:T(8,128)(2,1)S(1)} custom-call(f32[40,64]{1,0:T(8,128)S(1)} %pad_select_fusion.t_ref, f32[8,4096,128]{2,1,0:T(8,128)} %bitcast.17, f32[8,16,128]{2,1,0:T(8,128)S(1)} %bitcast.16), custom_call_target="tpu_custom_call" | custom-call | flops 3221225472 | bytes 16777216 | tf_op jit(solution)/shard_map/spectra/pallas_call | solution.py:140
  14.7 37.7 %all_to_all.10.own_hbm = bf16[16,64,1024]{2,1,0:T(8,128)(2,1)} all-to-all(bf16[16,64,1024]{2,1,0:T(8,128)(2,1)S(1)} %spectra.1), channel_id=1, replica_groups=mesh['tm'=8,'chan'=16] {'chan'}, dimensions={0} | all-to-all | bytes 4194304 | tf_op jit(solution)/shard_map/all_to_all | solution.py:303
  52.4 0.4 collective-permute-start.1
  52.8 4.1 %own_products.1.p_ref = f32[4,1024,256]{2,1,0:T(8,128)S(1)} custom-call(s32[1]{0:T(128)} %bitcast.core_ref, bf16[16,64,1024]{2,1,0:T(8,128)(2,1)} %all_to_all.10.own_hbm), custom_call_target="tpu_custom_call" | custom-call | flops 2147483648 | bytes 6291456 | tf_op jit(solution)/shard_map/own_products/pallas_call | solution.py:209
  56.9 0.0 collective-permute-done.1.other_ref.columns_ref
  56.9 3.7 %product_codes.1 = s16[4,16,128,128]{3,2,1,0:T(8,128)(2,1)S(1)} custom-call(s32[1]{0:T(128)} %bitcast.core_ref, bf16[16,64,1024]{2,1,0:T(8,128)(2,1)S(1)} %collective-permute-done.1.other_ref.columns_ref, bf16[16,64,1024]{2,1,0:T(8,128)(2,1)S(1)} %collective-permute-done.1.other_ref.columns_ref, f32[4,1024,256]{2,1,0:T(8,128)S(1)} %own_products.1.p_ref), custom_call_target="tpu_custom_call" | custom-call | flops 2147483648 | bytes 8388608 | tf_op jit(solution)/shard_map/product_codes/pallas_call | solution.py:234
  60.7 38.3 %all_to_all.11 = s16[64,128,128]{2,1,0:T(8,128)(2,1)S(1)} all-to-all(s16[64,128,128]{2,1,0:T(8,128)(2,1)S(1)} %bitcast.15), channel_id=1, replica_groups={{0,1,2,3,4,5,6,7,8,9,10,11,12,13,14,15,32,33,34,35,36,37,38,39,40,41,42..., dimensions={0} | all-to-all | bytes 4194304 | tf_op jit(solution)/shard_map/all_to_all | solution.py:309
  98.9 2.3 %total.1 = f32[2,16,64,128]{3,2,1,0:T(8,128)} custom-call(s16[4,16,128,128]{3,2,1,0:T(8,128)(2,1)S(1)} %bitcast.14), custom_call_target="tpu_custom_call" | custom-call | flops 6291456 | bytes 3145728 | tf_op jit(solution)/shard_map/total/pallas_call | solution.py:279
  (2 shorter events, 0.0 us)
Async XLA Ops:
  0.8 2.8 %collective-permute-start = (f32[64,256]{1,0:T(8,128)S(1)}, f32[64,256]{1,0:T(8,128)S(1)}, u32[]{:S(2)}, u32[]{:S(2)}) collective-permute-start(f32[64,256]{1,0:T(8,128)S(1)} %slice.3), channel_id=1, source_target_pairs={{0,16},{16,32},{32,48},{48,64},{64,80},{80,96},{96,112},{1,17},{17... | collective-permute-start | bytes 196616 | tf_op jit(solution)/shard_map/ppermute | solution.py:21
  52.4 4.5 %collective-permute-start.1 = (bf16[16,64,1024]{2,1,0:T(8,128)(2,1)}, bf16[16,64,1024]{2,1,0:T(8,128)(2,1)S(1)}, u32[]{:S(2)}, u32[]{:S(2)}) collective-permute-start(bf16[16,64,1024]{2,1,0:T(8,128)(2,1)} %all_to_all.10.own_hbm), channel_id=1, source_target_pairs={{0,16},{16,0},{32,48},{48,32},{64,80},{80,64},{96,112},{112,96},{1... | collective-permute-start | bytes 6291464 | tf_op jit(solution)/shard_map/ppermute | solution.py:304

commit v5 on v4

--- a/solution.py
+++ b/solution.py
@@ -259,14 +259,14 @@
         total = jnp.zeros((2 * width, HOP), jnp.float32)
         for y in range(blocks):
             code = c_ref[y, b].astype(jnp.int32).astype(jnp.float32)
-            level = jnp.abs(code) * (1.0 / STEPS) + math.log2(LEAST * scale)
-            size = jnp.exp2(level)
-            total = total + jnp.where(code > 0.0, size, jnp.where(code < 0.0, -size, 0.0))
+            size = jnp.exp2(jnp.abs(code) * (1.0 / STEPS))
+            total = total + jnp.where(code < 0.0, 1.0 - size, size - 1.0)
+        total = total * (LEAST * scale)
         buf[0, b] = total[:width]
         buf[1, b] = total[width:]
-        if b % 2 == 1:
-            both = pl.ds(b - 1, 2)
-            copy = pltpu.make_async_copy(buf.at[:, both], o_ref.at[:, both], sems.at[b // 2])
+        if b % 4 == 3:
+            done = pl.ds(b - 3, 4)
+            copy = pltpu.make_async_copy(buf.at[:, done], o_ref.at[:, done], sems.at[b // 4])
             copy.start()
             copies.append(copy)
     for copy in copies:
@@ -283,7 +283,7 @@
         out_shape=jax.ShapeDtypeStruct((2, nbin, width, HOP), jnp.float32),
         scratch_shapes=[
             pltpu.VMEM((2, nbin, width, HOP), jnp.float32),
-            pltpu.SemaphoreType.DMA((nbin // 2,)),
+            pltpu.SemaphoreType.DMA((nbin // 4,)),
         ],
         compiler_params=pltpu.CompilerParams(vmem_limit_bytes=32 * 2**20),
         cost_estimate=pl.CostEstimate(

time: 102 us -> 102 us (level)
  no operation moved by 1% of the time
where the time goes in v5:
time: 102 us; the launch traced here: 101 us
  blocking collectives  76 us (75%)
  Pallas kernels  21 us (21%)
  starting transfers between devices  1.66 us (2%)
  other arithmetic  1.46 us (1%)
    all_to_all x1, blocking collectives, body(): lax.all_to_all(codes.reshape(times // 2 * chans, height, HOP), ('tm', 'ch...  38.3 us
    all_to_all x1, blocking collectives, body(): mine = lax.all_to_all(own, 'chan', 0, 0)  37.7 us
    pallas_call x1, Pallas kernels, spectra(): pl.pallas_call(spectra_kernel, in_specs=[pl.BlockSpec(memory_space=pltpu....  11.1 us
    pallas_call x1, Pallas kernels, own_products(): pl.pallas_call(own_kernel, in_specs=[pl.BlockSpec(memory_space=pltpu.SMEM...  4.1 us
    pallas_call x1, Pallas kernels, product_codes(): pl.pallas_call(code_kernel, in_specs=[pl.BlockSpec(memory_space=pltpu.SME...  3.73 us
    pallas_call x1, Pallas kernels, total_of(): pl.pallas_call(functools.partial(total_kernel, scale), in_specs=[pl.Block...  2.09 us
  transfers between devices with their start and end apart: 2, of which 0 were waited for; matrix products, arithmetic and copies ran while one was open for 1% of the time, Pallas kernels for 4%

profile of v5, /device:TPU:0, one launch (start us, length us, event | category | flops | bytes accessed | tf_op | source)
XLA Modules:
  0.0 101.2 jit_solution(17378411608886002757)
XLA Ops:
  0.0 0.8 slice.3
  0.8 1.3 %collective-permute-start = (f32[64,256]{1,0:T(8,128)S(1)}, f32[64,256]{1,0:T(8,128)S(1)}, u32[]{:S(2)}, u32[]{:S(2)}) collective-permute-start(f32[64,256]{1,0:T(8,128)S(1)} %slice.3), channel_id=1, source_target_pairs={{0,16},{16,32},{32,48},{48,64},{64,80},{80,96},{96,112},{1,17},{17... | collective-permute-start | bytes 196616 | tf_op jit(solution)/shard_map/ppermute | solution.py:21
  2.1 0.7 convert_element_type.7
  2.8 0.8 pad_select_fusion.t_ref
  3.6 0.0 collective-permute-done
  3.6 11.1 %spectra.1 = bf16[16,64,1024]{2,1,0:T(8,128)(2,1)S(1)} custom-call(f32[40,64]{1,0:T(8,128)S(1)} %pad_select_fusion.t_ref, f32[8,4096,128]{2,1,0:T(8,128)} %bitcast.17, f32[8,16,128]{2,1,0:T(8,128)S(1)} %bitcast.16), custom_call_target="tpu_custom_call" | custom-call | flops 3221225472 | bytes 16777216 | tf_op jit(solution)/shard_map/spectra/pallas_call | solution.py:140
  14.7 37.7 %all_to_all.10.own_hbm = bf16[16,64,1024]{2,1,0:T(8,128)(2,1)} all-to-all(bf16[16,64,1024]{2,1,0:T(8,128)(2,1)S(1)} %spectra.1), channel_id=1, replica_groups=mesh['tm'=8,'chan'=16] {'chan'}, dimensions={0} | all-to-all | bytes 4194304 | tf_op jit(solution)/shard_map/all_to_all | solution.py:303
  52.4 0.4 collective-permute-start.1
  52.8 4.1 %own_products.1.p_ref = f32[4,1024,256]{2,1,0:T(8,128)S(1)} custom-call(s32[1]{0:T(128)} %bitcast.core_ref, bf16[16,64,1024]{2,1,0:T(8,128)(2,1)} %all_to_all.10.own_hbm), custom_call_target="tpu_custom_call" | custom-call | flops 2147483648 | bytes 6291456 | tf_op jit(solution)/shard_map/own_products/pallas_call | solution.py:209
  56.9 0.0 collective-permute-done.1.other_ref.columns_ref
  56.9 3.7 %product_codes.1 = s16[4,16,128,128]{3,2,1,0:T(8,128)(2,1)S(1)} custom-call(s32[1]{0:T(128)} %bitcast.core_ref, bf16[16,64,1024]{2,1,0:T(8,128)(2,1)S(1)} %collective-permute-done.1.other_ref.columns_ref, bf16[16,64,1024]{2,1,0:T(8,128)(2,1)S(1)} %collective-permute-done.1.other_ref.columns_ref, f32[4,1024,256]{2,1,0:T(8,128)S(1)} %own_products.1.p_ref), custom_call_target="tpu_custom_call" | custom-call | flops 2147483648 | bytes 8388608 | tf_op jit(solution)/shard_map/product_codes/pallas_call | solution.py:234
  60.7 38.3 %all_to_all.11 = s16[64,128,128]{2,1,0:T(8,128)(2,1)S(1)} all-to-all(s16[64,128,128]{2,1,0:T(8,128)(2,1)S(1)} %bitcast.15), channel_id=1, replica_groups={{0,1,2,3,4,5,6,7,8,9,10,11,12,13,14,15,32,33,34,35,36,37,38,39,40,41,42..., dimensions={0} | all-to-all | bytes 4194304 | tf_op jit(solution)/shard_map/all_to_all | solution.py:309
  98.9 2.1 %total.1 = f32[2,16,64,128]{3,2,1,0:T(8,128)} custom-call(s16[4,16,128,128]{3,2,1,0:T(8,128)(2,1)S(1)} %bitcast.14), custom_call_target="tpu_custom_call" | custom-call | flops 6291456 | bytes 3145728 | tf_op jit(solution)/shard_map/total/pallas_call | solution.py:279
  (2 shorter events, 0.0 us)
Async XLA Ops:
  0.8 2.8 %collective-permute-start = (f32[64,256]{1,0:T(8,128)S(1)}, f32[64,256]{1,0:T(8,128)S(1)}, u32[]{:S(2)}, u32[]{:S(2)}) collective-permute-start(f32[64,256]{1,0:T(8,128)S(1)} %slice.3), channel_id=1, source_target_pairs={{0,16},{16,32},{32,48},{48,64},{64,80},{80,96},{96,112},{1,17},{17... | collective-permute-start | bytes 196616 | tf_op jit(solution)/shard_map/ppermute | solution.py:21
  52.4 4.5 %collective-permute-start.1 = (bf16[16,64,1024]{2,1,0:T(8,128)(2,1)}, bf16[16,64,1024]{2,1,0:T(8,128)(2,1)S(1)}, u32[]{:S(2)}, u32[]{:S(2)}) collective-permute-start(bf16[16,64,1024]{2,1,0:T(8,128)(2,1)} %all_to_all.10.own_hbm), channel_id=1, source_target_pairs={{0,16},{16,0},{32,48},{48,32},{64,80},{80,64},{96,112},{112,96},{1... | collective-permute-start | bytes 6291464 | tf_op jit(solution)/shard_map/ppermute | solution.py:304

commit v6 on v5

--- a/solution.py
+++ b/solution.py
@@ -176,6 +176,11 @@
     return lax.dot_general(rows, columns, NT, preferred_element_type=jnp.float32)
 
 
+def reversed_bits(count):
+    bits = count.bit_length() - 1
+    return [sum((i >> k & 1) << (bits - 1 - k) for k in range(bits)) for i in range(count)]
+
+
 def own_kernel(core_ref, own_hbm, p_ref, own_ref, sems):
     nsrc, width, _ = own_ref.shape
     copies = [pltpu.make_async_copy(own_hbm.at[r], own_ref.at[r], sems.at[r]) for r in range(nsrc)]
@@ -191,6 +196,7 @@
 
 def code_kernel(core_ref, other_ref, columns_ref, p_ref, o_ref):
     nsrc, width, _ = other_ref.shape
+    place = reversed_bits(o_ref.shape[0])
     for y in range(p_ref.shape[0]):
         other = columns_of(columns_ref, y, core_ref[0])
         for r in range(0, nsrc, 4):
@@ -199,8 +205,10 @@
             code = (level * STEPS + (0.5 - math.log2(LEAST) * STEPS)).astype(jnp.int32)
             code = jnp.where(part < 0.0, -code, code).astype(jnp.int16)
             code = code.reshape(4, width, 2 * HOP)
-            o_ref[y, r : r + 4, :width] = code[:, :, :HOP]
-            o_ref[y, r : r + 4, width:] = code[:, :, HOP:]
+            for i in range(4):
+                at = place[y * nsrc + r + i]
+                o_ref[at, :width] = code[i, :, :HOP]
+                o_ref[at, width:] = code[i, :, HOP:]
 
 
 def own_products(core, own, blocks):
@@ -240,7 +248,7 @@
             pl.BlockSpec(memory_space=pltpu.VMEM),
         ],
         out_specs=pl.BlockSpec(memory_space=pltpu.VMEM),
-        out_shape=jax.ShapeDtypeStruct((blocks, nsrc, 2 * width, HOP), jnp.int16),
+        out_shape=jax.ShapeDtypeStruct((blocks * nsrc, 2 * width, HOP), jnp.int16),
         compiler_params=pltpu.CompilerParams(vmem_limit_bytes=32 * 2**20),
         cost_estimate=pl.CostEstimate(
             flops=4 * chans * blocks * HOP * depth,
@@ -252,13 +260,14 @@
 
 
 def total_kernel(scale, c_ref, o_ref, buf, sems):
-    blocks, nbin, _, _ = c_ref.shape
-    width = buf.shape[2]
+    _, nbin, width, _ = buf.shape
+    blocks = c_ref.shape[0] // nbin
+    place = reversed_bits(blocks * nbin)
     copies = []
     for b in range(nbin):
         total = jnp.zeros((2 * width, HOP), jnp.float32)
         for y in range(blocks):
-            code = c_ref[y, b].astype(jnp.int32).astype(jnp.float32)
+            code = c_ref[place[y * nbin + b]].astype(jnp.int32).astype(jnp.float32)
             size = jnp.exp2(jnp.abs(code) * (1.0 / STEPS))
             total = total + jnp.where(code < 0.0, 1.0 - size, size - 1.0)
         total = total * (LEAST * scale)
@@ -273,8 +282,9 @@
         copy.wait()
 
 
-def total_of(codes, scale):
-    blocks, nbin, height, _ = codes.shape
+def total_of(codes, nbin, scale):
+    count, height, _ = codes.shape
+    blocks = count // nbin
     width = height // 2
     return pl.pallas_call(
         functools.partial(total_kernel, scale),
@@ -304,17 +314,13 @@
     other = lax.ppermute(mine, "tm", [(i, i ^ 1) for i in range(times)])
     core = (lax.axis_index("tm") % 2).astype(jnp.int32).reshape(1)
     codes = product_codes(core, other, own_products(core, mine, times // 2))
-    height = codes.shape[2]
-    same_core = [[t * chans + c for t in range(h, times, 2) for c in range(chans)] for h in range(2)]
-    codes = lax.all_to_all(
-        codes.reshape(times // 2 * chans, height, HOP),
-        ("tm", "chan"),
-        0,
-        0,
-        axis_index_groups=same_core,
-    )
+    same_core = [
+        [(2 * (i // chans) + h) * chans + i % chans for i in reversed_bits(times // 2 * chans)]
+        for h in range(2)
+    ]
+    codes = lax.all_to_all(codes, ("tm", "chan"), 0, 0, axis_index_groups=same_core)
     scale = 1.0 / (times * (span // HOP) * 3.0 * SEG / 8.0)
-    return total_of(codes.reshape(times // 2, chans, height, HOP), scale)
+    return total_of(codes, chans, scale)
 
 
 def solution(mesh):

time: 102 us -> 100 us (0.980)
  blocking collectives: 76 us -> 74.3 us
    all_to_all x1, blocking collectives: 38.3 us -> 36.6 us  [body(): lax.all_to_all(codes, ('tm', 'chan'), 0, 0, axis_index_groups=same_core)]
where the time goes in v6:
time: 100 us; the launch traced here: 99.5 us
  blocking collectives  74.3 us (74%)
  Pallas kernels  21 us (21%)
  starting transfers between devices  1.66 us (2%)
  other arithmetic  1.46 us (1%)
    all_to_all x1, blocking collectives, body(): mine = lax.all_to_all(own, 'chan', 0, 0)  37.7 us
    all_to_all x1, blocking collectives, body(): lax.all_to_all(codes, ('tm', 'chan'), 0, 0, axis_index_groups=same_core)  36.6 us
    pallas_call x1, Pallas kernels, spectra(): pl.pallas_call(spectra_kernel, in_specs=[pl.BlockSpec(memory_space=pltpu....  11.1 us
    pallas_call x1, Pallas kernels, own_products(): pl.pallas_call(own_kernel, in_specs=[pl.BlockSpec(memory_space=pltpu.SMEM...  4.1 us
    pallas_call x1, Pallas kernels, product_codes(): pl.pallas_call(code_kernel, in_specs=[pl.BlockSpec(memory_space=pltpu.SME...  3.73 us
    pallas_call x1, Pallas kernels, total_of(): pl.pallas_call(functools.partial(total_kernel, scale), in_specs=[pl.Block...  2.09 us
  transfers between devices with their start and end apart: 2, of which 0 were waited for; matrix products, arithmetic and copies ran while one was open for 1% of the time, Pallas kernels for 4%

profile of v6, /device:TPU:0, one launch (start us, length us, event | category | flops | bytes accessed | tf_op | source)
XLA Modules:
  0.0 99.5 jit_solution(4738153450234292538)
XLA Ops:
  0.0 0.8 slice.3
  0.8 1.3 %collective-permute-start = (f32[64,256]{1,0:T(8,128)S(1)}, f32[64,256]{1,0:T(8,128)S(1)}, u32[]{:S(2)}, u32[]{:S(2)}) collective-permute-start(f32[64,256]{1,0:T(8,128)S(1)} %slice.3), channel_id=1, source_target_pairs={{0,16},{16,32},{32,48},{48,64},{64,80},{80,96},{96,112},{1,17},{17... | collective-permute-start | bytes 196616 | tf_op jit(solution)/shard_map/ppermute | solution.py:21
  2.1 0.7 convert_element_type.7
  2.8 0.8 pad_select_fusion.t_ref
  3.6 0.0 collective-permute-done
  3.6 11.1 %spectra.1 = bf16[16,64,1024]{2,1,0:T(8,128)(2,1)S(1)} custom-call(f32[40,64]{1,0:T(8,128)S(1)} %pad_select_fusion.t_ref, f32[8,4096,128]{2,1,0:T(8,128)} %bitcast.13, f32[8,16,128]{2,1,0:T(8,128)S(1)} %bitcast.12), custom_call_target="tpu_custom_call" | custom-call | flops 3221225472 | bytes 16777216 | tf_op jit(solution)/shard_map/spectra/pallas_call | solution.py:140
  14.7 37.7 %all_to_all.10.own_hbm = bf16[16,64,1024]{2,1,0:T(8,128)(2,1)} all-to-all(bf16[16,64,1024]{2,1,0:T(8,128)(2,1)S(1)} %spectra.1), channel_id=1, replica_groups=mesh['tm'=8,'chan'=16] {'chan'}, dimensions={0} | all-to-all | bytes 4194304 | tf_op jit(solution)/shard_map/all_to_all | solution.py:313
  52.4 0.4 collective-permute-start.1
  52.8 4.1 %own_products.1.p_ref = f32[4,1024,256]{2,1,0:T(8,128)S(1)} custom-call(s32[1]{0:T(128)} %bitcast.core_ref, bf16[16,64,1024]{2,1,0:T(8,128)(2,1)} %all_to_all.10.own_hbm), custom_call_target="tpu_custom_call" | custom-call | flops 2147483648 | bytes 6291456 | tf_op jit(solution)/shard_map/own_products/pallas_call | solution.py:217
  56.9 0.0 collective-permute-done.1.other_ref.columns_ref
  56.9 3.7 %product_codes.1 = s16[64,128,128]{2,1,0:T(8,128)(2,1)S(1)} custom-call(s32[1]{0:T(128)} %bitcast.core_ref, bf16[16,64,1024]{2,1,0:T(8,128)(2,1)S(1)} %collective-permute-done.1.other_ref.columns_ref, bf16[16,64,1024]{2,1,0:T(8,128)(2,1)S(1)} %collective-permute-done.1.other_ref.columns_ref, f32[4,1024,256]{2,1,0:T(8,128)S(1)} %own_products.1.p_ref), custom_call_target="tpu_custom_call" | custom-call | flops 2147483648 | bytes 8388608 | tf_op jit(solution)/shard_map/product_codes/pallas_call | solution.py:242
  60.7 36.6 %all_to_all.11.c_ref = s16[64,128,128]{2,1,0:T(8,128)(2,1)S(1)} all-to-all(s16[64,128,128]{2,1,0:T(8,128)(2,1)S(1)} %product_codes.1), channel_id=1, replica_groups={{0,64,32,96,8,72,40,104,4,68,36,100,12,76,44,108,2,66,34,98,10,74,42,10..., dimensions={0} | all-to-all | bytes 4194304 | tf_op jit(solution)/shard_map/all_to_all | solution.py:321
  97.3 2.1 %total.1 = f32[2,16,64,128]{3,2,1,0:T(8,128)} custom-call(s16[64,128,128]{2,1,0:T(8,128)(2,1)S(1)} %all_to_all.11.c_ref), custom_call_target="tpu_custom_call" | custom-call | flops 6291456 | bytes 3145728 | tf_op jit(solution)/shard_map/total/pallas_call | solution.py:289
  (2 shorter events, 0.0 us)
Async XLA Ops:
  0.8 2.8 %collective-permute-start = (f32[64,256]{1,0:T(8,128)S(1)}, f32[64,256]{1,0:T(8,128)S(1)}, u32[]{:S(2)}, u32[]{:S(2)}) collective-permute-start(f32[64,256]{1,0:T(8,128)S(1)} %slice.3), channel_id=1, source_target_pairs={{0,16},{16,32},{32,48},{48,64},{64,80},{80,96},{96,112},{1,17},{17... | collective-permute-start | bytes 196616 | tf_op jit(solution)/shard_map/ppermute | solution.py:21
  52.4 4.5 %collective-permute-start.1 = (bf16[16,64,1024]{2,1,0:T(8,128)(2,1)}, bf16[16,64,1024]{2,1,0:T(8,128)(2,1)S(1)}, u32[]{:S(2)}, u32[]{:S(2)}) collective-permute-start(bf16[16,64,1024]{2,1,0:T(8,128)(2,1)} %all_to_all.10.own_hbm), channel_id=1, source_target_pairs={{0,16},{16,0},{32,48},{48,32},{64,80},{80,64},{96,112},{112,96},{1... | collective-permute-start | bytes 6291464 | tf_op jit(solution)/shard_map/ppermute | solution.py:314

commit v7 on v6

--- a/solution.py
+++ b/solution.py
@@ -176,9 +176,15 @@
     return lax.dot_general(rows, columns, NT, preferred_element_type=jnp.float32)
 
 
-def reversed_bits(count):
+def spread_order(count):
     bits = count.bit_length() - 1
-    return [sum((i >> k & 1) << (bits - 1 - k) for k in range(bits)) for i in range(count)]
+    taken = [*range(bits - 1, -1, -2), *range(bits - 2, -1, -2)]
+    return [sum((p >> k & 1) << taken[k] for k in range(bits)) for p in range(count)]
+
+
+def places(count):
+    order = spread_order(count)
+    return [order.index(i) for i in range(count)]
 
 
 def own_kernel(core_ref, own_hbm, p_ref, own_ref, sems):
@@ -196,7 +202,7 @@
 
 def code_kernel(core_ref, other_ref, columns_ref, p_ref, o_ref):
     nsrc, width, _ = other_ref.shape
-    place = reversed_bits(o_ref.shape[0])
+    place = places(o_ref.shape[0])
     for y in range(p_ref.shape[0]):
         other = columns_of(columns_ref, y, core_ref[0])
         for r in range(0, nsrc, 4):
@@ -262,7 +268,7 @@
 def total_kernel(scale, c_ref, o_ref, buf, sems):
     _, nbin, width, _ = buf.shape
     blocks = c_ref.shape[0] // nbin
-    place = reversed_bits(blocks * nbin)
+    place = places(blocks * nbin)
     copies = []
     for b in range(nbin):
         total = jnp.zeros((2 * width, HOP), jnp.float32)
@@ -315,7 +321,7 @@
     core = (lax.axis_index("tm") % 2).astype(jnp.int32).reshape(1)
     codes = product_codes(core, other, own_products(core, mine, times // 2))
     same_core = [
-        [(2 * (i // chans) + h) * chans + i % chans for i in reversed_bits(times // 2 * chans)]
+        [(2 * (i // chans) + h) * chans + i % chans for i in spread_order(times // 2 * chans)]
         for h in range(2)
     ]
     codes = lax.all_to_all(codes, ("tm", "chan"), 0, 0, axis_index_groups=same_core)

time: 100 us -> 101 us (1.010)
  blocking collectives: 74.3 us -> 75.5 us
    all_to_all x1, blocking collectives: 36.6 us -> 37.8 us  [body(): lax.all_to_all(codes, ('tm', 'chan'), 0, 0, axis_index_groups=same_core)]
where the time goes in v7:
time: 101 us
  blocking collectives  75.5 us (75%)
  Pallas kernels  21 us (21%)
  starting transfers between devices  1.66 us (2%)
  other arithmetic  1.46 us (1%)
    all_to_all x1, blocking collectives, body(): lax.all_to_all(codes, ('tm', 'chan'), 0, 0, axis_index_groups=same_core)  37.8 us
    all_to_all x1, blocking collectives, body(): mine = lax.all_to_all(own, 'chan', 0, 0)  37.7 us
    pallas_call x1, Pallas kernels, spectra(): pl.pallas_call(spectra_kernel, in_specs=[pl.BlockSpec(memory_space=pltpu....  11.1 us
    pallas_call x1, Pallas kernels, own_products(): pl.pallas_call(own_kernel, in_specs=[pl.BlockSpec(memory_space=pltpu.SMEM...  4.1 us
    pallas_call x1, Pallas kernels, product_codes(): pl.pallas_call(code_kernel, in_specs=[pl.BlockSpec(memory_space=pltpu.SME...  3.73 us
    pallas_call x1, Pallas kernels, total_of(): pl.pallas_call(functools.partial(total_kernel, scale), in_specs=[pl.Block...  2.09 us
  transfers between devices with their start and end apart: 2, of which 0 were waited for; matrix products, arithmetic and copies ran while one was open for 1% of the time, Pallas kernels for 4%

profile of v7, /device:TPU:0, one launch (start us, length us, event | category | flops | bytes accessed | tf_op | source)
XLA Modules:
  0.0 100.7 jit_solution(11758126368428975129)
XLA Ops:
  0.0 0.8 slice.3
  0.8 1.3 %collective-permute-start = (f32[64,256]{1,0:T(8,128)S(1)}, f32[64,256]{1,0:T(8,128)S(1)}, u32[]{:S(2)}, u32[]{:S(2)}) collective-permute-start(f32[64,256]{1,0:T(8,128)S(1)} %slice.3), channel_id=1, source_target_pairs={{0,16},{16,32},{32,48},{48,64},{64,80},{80,96},{96,112},{1,17},{17... | collective-permute-start | bytes 196616 | tf_op jit(solution)/shard_map/ppermute | solution.py:21
  2.1 0.7 convert_element_type.7
  2.8 0.8 pad_select_fusion.t_ref
  3.6 0.0 collective-permute-done
  3.6 11.1 %spectra.1 = bf16[16,64,1024]{2,1,0:T(8,128)(2,1)S(1)} custom-call(f32[40,64]{1,0:T(8,128)S(1)} %pad_select_fusion.t_ref, f32[8,4096,128]{2,1,0:T(8,128)} %bitcast.13, f32[8,16,128]{2,1,0:T(8,128)S(1)} %bitcast.12), custom_call_target="tpu_custom_call" | custom-call | flops 3221225472 | bytes 16777216 | tf_op jit(solution)/shard_map/spectra/pallas_call | solution.py:140
  14.7 37.7 %all_to_all.10.own_hbm = bf16[16,64,1024]{2,1,0:T(8,128)(2,1)} all-to-all(bf16[16,64,1024]{2,1,0:T(8,128)(2,1)S(1)} %spectra.1), channel_id=1, replica_groups=mesh['tm'=8,'chan'=16] {'chan'}, dimensions={0} | all-to-all | bytes 4194304 | tf_op jit(solution)/shard_map/all_to_all | solution.py:319
  52.4 0.4 collective-permute-start.1
  52.8 4.1 %own_products.1.p_ref = f32[4,1024,256]{2,1,0:T(8,128)S(1)} custom-call(s32[1]{0:T(128)} %bitcast.core_ref, bf16[16,64,1024]{2,1,0:T(8,128)(2,1)} %all_to_all.10.own_hbm), custom_call_target="tpu_custom_call" | custom-call | flops 2147483648 | bytes 6291456 | tf_op jit(solution)/shard_map/own_products/pallas_call | solution.py:223
  56.9 0.0 collective-permute-done.1.other_ref.columns_ref
  56.9 3.7 %product_codes.1 = s16[64,128,128]{2,1,0:T(8,128)(2,1)S(1)} custom-call(s32[1]{0:T(128)} %bitcast.core_ref, bf16[16,64,1024]{2,1,0:T(8,128)(2,1)S(1)} %collective-permute-done.1.other_ref.columns_ref, bf16[16,64,1024]{2,1,0:T(8,128)(2,1)S(1)} %collective-permute-done.1.other_ref.columns_ref, f32[4,1024,256]{2,1,0:T(8,128)S(1)} %own_products.1.p_ref), custom_call_target="tpu_custom_call" | custom-call | flops 2147483648 | bytes 8388608 | tf_op jit(solution)/shard_map/product_codes/pallas_call | solution.py:248
  60.7 37.8 %all_to_all.11.c_ref = s16[64,128,128]{2,1,0:T(8,128)(2,1)S(1)} all-to-all(s16[64,128,128]{2,1,0:T(8,128)(2,1)S(1)} %product_codes.1), channel_id=1, replica_groups={{0,64,8,72,2,66,10,74,32,96,40,104,34,98,42,106,4,68,12,76,6,70,14,78,3..., dimensions={0} | all-to-all | bytes 4194304 | tf_op jit(solution)/shard_map/all_to_all | solution.py:327
  98.4 2.1 %total.1 = f32[2,16,64,128]{3,2,1,0:T(8,128)} custom-call(s16[64,128,128]{2,1,0:T(8,128)(2,1)S(1)} %all_to_all.11.c_ref), custom_call_target="tpu_custom_call" | custom-call | flops 6291456 | bytes 3145728 | tf_op jit(solution)/shard_map/total/pallas_call | solution.py:295
  (2 shorter events, 0.0 us)
Async XLA Ops:
  0.8 2.8 %collective-permute-start = (f32[64,256]{1,0:T(8,128)S(1)}, f32[64,256]{1,0:T(8,128)S(1)}, u32[]{:S(2)}, u32[]{:S(2)}) collective-permute-start(f32[64,256]{1,0:T(8,128)S(1)} %slice.3), channel_id=1, source_target_pairs={{0,16},{16,32},{32,48},{48,64},{64,80},{80,96},{96,112},{1,17},{17... | collective-permute-start | bytes 196616 | tf_op jit(solution)/shard_map/ppermute | solution.py:21
  52.4 4.5 %collective-permute-start.1 = (bf16[16,64,1024]{2,1,0:T(8,128)(2,1)}, bf16[16,64,1024]{2,1,0:T(8,128)(2,1)S(1)}, u32[]{:S(2)}, u32[]{:S(2)}) collective-permute-start(bf16[16,64,1024]{2,1,0:T(8,128)(2,1)} %all_to_all.10.own_hbm), channel_id=1, source_target_pairs={{0,16},{16,0},{32,48},{48,32},{64,80},{80,64},{96,112},{112,96},{1... | collective-permute-start | bytes 6291464 | tf_op jit(solution)/shard_map/ppermute | solution.py:320
